TPU v7x, 256 devices: a whole 4x4x8 slice. The times are simulated.
256 devices in a mesh: ray: 64 (over x, z, core), row: 4 (over y).
Axes of the slice: x: 4, y: 4, z: 8, core: 2. Of those that a mesh axis runs over, the one named last changes fastest.
Arguments:
- density: float32 [2048, 64, 1024], P('ray', 'row'), may hold values from 0.2 to 5
- light_dir: float32 [3], replicated, may hold values from -1 to 1
- colour_tint: float32 [3], replicated, may hold values from 0.5 to 2
- cotangent: float32 [3, 64, 1024], P(None, 'row'), may hold values from -6 to 6
Outputs:
- dens_grad: float32 [2048, 64, 1024], P('ray', 'row')
All inputs are finite; a program needn't handle non-finite values.
Results may differ from a plain program's by a relative error of at most 0.0003.
Values sent between devices are 32-bit elements; how exact they have to be, the bound alone decides.
No kernel may reach another device: no remote copies, remote signals or barrier semaphores. Data moves between devices by JAX's collectives and lax.ppermute only.
A program may use at most 128 MiB of HBM per device.

v0:
```python
import jax
import jax.numpy as jnp
from jax import lax
from jax.sharding import Mesh
from jax.sharding import PartitionSpec as P

RAY = ("ray_0", "ray_1", "ray_2")


EXTINCTION = 0.7


def with_halo(cells, sides, width):
    for axis, dim in sides:
        count = lax.axis_size(axis)
        ends = count - 1
        head = lax.slice_in_dim(cells, 0, width, axis=dim)
        tail = lax.slice_in_dim(cells, cells.shape[dim] - width, cells.shape[dim], axis=dim)
        cells = jnp.concatenate(
            [
                lax.ppermute(tail, axis, [(i, (i + 1) % count) for i in range(ends)]),
                cells,
                lax.ppermute(head, axis, [((i + 1) % count, i) for i in range(ends)]),
            ],
            axis=dim,
        )
    return cells


def nothing_yet(value, identity):
    return jax.tree.map(
        lambda part, zero: jnp.zeros_like(part) + jnp.asarray(zero, part.dtype), value, identity
    )


def prefix_by_axis(value, axes, combine, identity, reverse):
    before = start = nothing_yet(value, identity)
    subtotal = value
    for axis in reversed(axes):
        devices, place = (lax.axis_size(axis), lax.axis_index(axis))
        pieces = jax.tree.map(lambda part: lax.all_gather(part, axis), subtotal)
        inside, subtotal = (start, start)
        for k in reversed(range(devices)) if reverse else range(devices):
            passed = k > place if reverse else k < place
            subtotal = combine(subtotal, jax.tree.map(lambda part: part[k], pieces))
            inside = jax.tree.map(lambda new, old: jnp.where(passed, new, old), subtotal, inside)
        before = combine(inside, before)
    return before


def over_combine(farther, nearer):
    far_depth, far_colour = farther
    near_depth, near_colour = nearer
    return (far_depth + near_depth, near_colour + jnp.exp(-near_depth) * far_colour)


def add_depths(earlier_depth, later_depth):
    return earlier_depth + later_depth


def column_diff(layer):
    col_padded = jnp.pad(layer, ((0, 0), (1, 1)))
    return (col_padded[:, 2:] - col_padded[:, :-2]) * 0.5


def rim_adjoint(rimmed, layer, trans_factor, projector, light_dir, depth_step):
    inner = rimmed[layer, 2:-2]
    grad_x = (rimmed[layer + 1, 2:-2] - rimmed[layer - 1, 2:-2]) * 0.5
    grad_y = (rimmed[layer, 3:-1] - rimmed[layer, 1:-3]) * 0.5
    grad_z = column_diff(inner)
    radius = jnp.sqrt(1.0 + grad_x * grad_x + grad_y * grad_y + grad_z * grad_z)
    lit = light_dir[0] * grad_x + light_dir[1] * grad_y + light_dir[2] * grad_z
    opacity = 1.0 - jnp.exp(-(inner * depth_step))
    adj_shading = trans_factor * opacity * inner * projector
    scaled = 0.5 * adj_shading / radius
    bent = scaled * lit / (radius * radius)
    return scaled * light_dir[0] - bent * grad_x


def local(density, light_dir, colour_tint, cotangent):
    depth_cells = density.shape[0]
    full_depth = depth_cells * lax.axis_size(RAY)
    depth_step = EXTINCTION / full_depth
    optical = density * depth_step
    slab_depth = jnp.sum(optical, axis=0)
    local_trans = jnp.exp(-(jnp.cumsum(optical, axis=0) - optical))
    passing = jnp.exp(-optical)
    opacity = 1.0 - passing
    rimmed = with_halo(density, ((RAY, 0), ("row", 1)), 2)
    padded = rimmed[1:-1, 1:-1]
    grad_x = (padded[2:, 1:-1] - padded[:-2, 1:-1]) * 0.5
    grad_y = (padded[1:-1, 2:] - padded[1:-1, :-2]) * 0.5
    col_padded = jnp.pad(density, ((0, 0), (0, 0), (1, 1)))
    grad_z = (col_padded[:, :, 2:] - col_padded[:, :, :-2]) * 0.5
    radius = jnp.sqrt(1.0 + grad_x * grad_x + grad_y * grad_y + grad_z * grad_z)
    lit = light_dir[0] * grad_x + light_dir[1] * grad_y + light_dir[2] * grad_z
    shading = 0.5 + 0.5 * lit / radius
    emitted = local_trans * opacity * density * shading
    emitted_sum = jnp.sum(emitted, axis=0)
    projector = jnp.sum(cotangent * colour_tint[:, None, None], axis=0)
    slab_value = projector * emitted_sum
    behind_depth, behind_value = prefix_by_axis(
        (slab_depth, slab_value),
        RAY,
        over_combine,
        (jnp.zeros_like(slab_depth), jnp.zeros_like(slab_value)),
        True,
    )
    before_depth = prefix_by_axis(slab_depth, RAY, add_depths, jnp.zeros_like(slab_depth), False)
    front = jnp.exp(-before_depth)
    transmit = front[None] * local_trans
    suffix_local = emitted_sum[None] - jnp.cumsum(emitted, axis=0)
    suffix_value = front[None] * (
        projector[None] * suffix_local + (jnp.exp(-slab_depth) * behind_value)[None]
    )
    own_value = projector[None] * density * shading
    adj_optical = transmit * passing * own_value - suffix_value
    adj_shading = transmit * opacity * density * projector[None]
    adj_density = transmit * opacity * shading * projector[None] + adj_optical * depth_step
    scaled = 0.5 * adj_shading / radius
    bent = scaled * lit / (radius * radius)
    adj_x = scaled * light_dir[0] - bent * grad_x
    adj_y = scaled * light_dir[1] - bent * grad_y
    adj_z = scaled * light_dir[2] - bent * grad_z
    nearer_layer = rimmed[1, 2:-2] * depth_step
    lower_x = rim_adjoint(
        rimmed, 1, front * jnp.exp(nearer_layer), projector, light_dir, depth_step
    )
    upper_x = rim_adjoint(
        rimmed, depth_cells + 2, front * jnp.exp(-slab_depth), projector, light_dir, depth_step
    )
    halo_x = jnp.concatenate([lower_x[None], adj_x, upper_x[None]], axis=0)
    halo_y = with_halo(adj_y, (("row", 1),), 1)
    padded_z = jnp.pad(adj_z, ((0, 0), (0, 0), (1, 1)))
    adj_density = adj_density + (halo_x[:-2] - halo_x[2:]) * 0.5
    adj_density = adj_density + (halo_y[:, :-2] - halo_y[:, 2:]) * 0.5
    adj_density = adj_density + (padded_z[:, :, :-2] - padded_z[:, :, 2:]) * 0.5
    return adj_density * float(full_depth)


def solution(mesh):
    torus = Mesh(
        mesh.devices.reshape(4, 8, 2, mesh.shape["row"]), ("ray_0", "ray_1", "ray_2", "row")
    )
    placed = (P(RAY, "row", None), P(), P(), P(None, "row", None))
    return jax.shard_map(
        local, mesh=torus, in_specs=placed, out_specs=P(RAY, "row", None), check_vma=False
    )
```

profile of v0, /device:TPU:14, one launch (start us, length us, event | category | flops | bytes accessed | tf_op | source)
XLA Modules:
  0.0 149.8 jit_solution(12696540761980509998)
XLA Ops:
  1.0 7.5 %collective-permute-start = (f32[2,16,1024]{2,1,0:T(8,128)S(1)}, f32[2,16,1024]{2,1,0:T(8,128)S(1)}, u32[]{:S(2)}, u32[]{:S(2)}) collective-permute-start(f32[2,16,1024]{2,1,0:T(8,128)S(1)} %get-tuple-element.22), channel_id=1, source_target_pairs={{4,0},{8,4},{12,8},{16,12},{20,16},{24,20},{28,24},{32,28},{36,32}... | collective-permute-start | bytes 393224 | tf_op jit(solution)/shard_map/ppermute | solution.py:23
  8.5 1.9 %collective-permute-start.1 = (f32[2,16,1024]{2,1,0:T(8,128)S(1)}, f32[2,16,1024]{2,1,0:T(8,128)S(1)}, u32[]{:S(2)}, u32[]{:S(2)}) collective-permute-start(f32[2,16,1024]{2,1,0:T(8,128)S(1)} %get-tuple-element.23), channel_id=1, source_target_pairs={{0,4},{4,8},{8,12},{12,16},{16,20},{20,24},{24,28},{28,32},{32,36}... | collective-permute-start | bytes 393224 | tf_op jit(solution)/shard_map/ppermute | solution.py:21
  10.4 1.4 fusion.89
  13.6 1.0 multiply_reduce_fusion.1
  14.7 2.2 %collective-permute-done.1 = f32[2,16,1024]{2,1,0:T(8,128)S(1)} collective-permute-done((f32[2,16,1024]{2,1,0:T(8,128)S(1)}, f32[2,16,1024]{2,1,0:T(8,128)S(1)}, u32[]{:S(2)}, u32[]{:S(2)}) %collective-permute-start.1) | collective-permute-done | bytes 131104 | tf_op jit(solution)/shard_map/ppermute | solution.py:21
  16.9 1.9 %constant_dynamic-update-slice_fusion.1 = f32[36,16,1024]{2,1,0:T(8,128)S(1)} fusion(f32[36,16,1024]{2,1,0:T(8,128)S(1)} %constant_dynamic-update-slice_fusion.2, f32[32,16,1024]{2,1,0:T(8,128)} %param.4), kind=kLoop, calls=%fused_computation.162 | loop fusion | bytes 4194304
  19.1 2.4 %collective-permute-start.2 = (f32[36,2,1024]{2,1,0:T(2,128)S(1)}, f32[36,2,1024]{2,1,0:T(2,128)S(1)}, u32[]{:S(2)}, u32[]{:S(2)}) collective-permute-start(f32[36,2,1024]{2,1,0:T(2,128)S(1)} %get-tuple-element.17), channel_id=1, source_target_pairs={{1,0},{2,1},{3,2},{5,4},{6,5},{7,6},{9,8},{10,9},{11,10},{13,12},{... | collective-permute-start | bytes 884744 | tf_op jit(solution)/shard_map/ppermute | solution.py:23
  21.4 3.5 %collective-permute-start.3 = (f32[36,2,1024]{2,1,0:T(2,128)S(1)}, f32[36,2,1024]{2,1,0:T(2,128)S(1)}, u32[]{:S(2)}, u32[]{:S(2)}) collective-permute-start(f32[36,2,1024]{2,1,0:T(2,128)S(1)} %get-tuple-element.18), channel_id=1, source_target_pairs={{0,1},{1,2},{2,3},{4,5},{5,6},{6,7},{8,9},{9,10},{10,11},{12,13},{... | collective-permute-start | bytes 884744 | tf_op jit(solution)/shard_map/ppermute | solution.py:21
  25.0 2.7 %collective-permute-done.2 = f32[36,2,1024]{2,1,0:T(2,128)S(1)} collective-permute-done((f32[36,2,1024]{2,1,0:T(2,128)S(1)}, f32[36,2,1024]{2,1,0:T(2,128)S(1)}, u32[]{:S(2)}, u32[]{:S(2)}) %collective-permute-start.2) | collective-permute-done | bytes 294944 | tf_op jit(solution)/shard_map/ppermute | solution.py:23
  27.7 2.4 %collective-permute-done.3 = f32[36,2,1024]{2,1,0:T(2,128)S(1)} collective-permute-done((f32[36,2,1024]{2,1,0:T(2,128)S(1)}, f32[36,2,1024]{2,1,0:T(2,128)S(1)}, u32[]{:S(2)}, u32[]{:S(2)}) %collective-permute-start.3) | collective-permute-done | bytes 294944 | tf_op jit(solution)/shard_map/ppermute | solution.py:21
  30.1 5.2 %fusion.83 = (f32[16,1024]{1,0:T(8,128)S(1)}, f32[32,16,1024]{2,1,0:T(8,128)}, f32[32,16,1024]{2,1,0:T(8,128)S(1)}, f32[32,16,1024]{2,1,0:T(8,128)S(1)}, f32[32,...) fusion(f32[32,16,1024]{2,1,0:T(8,128)S(1)} %copy-done, f32[]{:T(128)S(6)} %mul.431, ...), kind=kOutput, calls=%fused_computation.165 | output fusion | flops 35094528 | bytes 18022412 | tf_op jit(solution)/shard_map/jit(cumsum)/reduce_window_sum | solution.py:86
  35.3 1.7 %fusion.90 = f32[32,16,1024]{2,1,0:T(8,128)S(1)} fusion(f32[32,16,1024]{2,1,0:T(8,128)} %get-tuple-element.8), kind=kOutput, calls=%fused_computation.170 | output fusion | flops 16252928 | bytes 4194304 | tf_op jit(solution)/shard_map/jit(cumsum)/reduce_window_sum | solution.py:112
  37.1 1.9 %all-gather.1 = f32[32,1024]{1,0:T(8,128)S(1)} all-gather(f32[16,1024]{1,0:T(8,128)S(1)} %mul.454), channel_id=3, replica_groups=mesh['ray_0'=4,'ray_1'=8,'ray_2'=2,'row'=4] {'ray_2'}, dimensions={0}, use_global_device_ids=true | all-gather | bytes 196608 | tf_op jit(solution)/shard_map/all_gather | solution.py:41
  39.0 1.9 %all-gather = f32[32,1024]{1,0:T(8,128)S(1)} all-gather(f32[16,1024]{1,0:T(8,128)S(1)} %get-tuple-element.21), channel_id=2, replica_groups=mesh['ray_0'=4,'ray_1'=8,'ray_2'=2,'row'=4] {'ray_2'}, dimensions={0}, use_global_device_ids=true | all-gather | bytes 196608 | tf_op jit(solution)/shard_map/all_gather | solution.py:41
  40.9 25.3 %all-gather.2 = f32[128,1024]{1,0:T(8,128)S(1)} all-gather(f32[16,1024]{1,0:T(8,128)S(1)} %get-tuple-element.27), channel_id=4, replica_groups=mesh['ray_0'=4,'ray_1'=8,'ray_2'=2,'row'=4] {'ray_1'}, dimensions={0}, use_global_device_ids=true | all-gather | bytes 589824 | tf_op jit(solution)/shard_map/all_gather | solution.py:41
  66.2 12.3 %all_gather.41 = f32[4,16,1024]{2,1,0:T(8,128)S(1)} all-gather(f32[1,16,1024]{2,1,0:T(8,128)S(1)} %get-tuple-element.24), channel_id=1, replica_groups=mesh['ray_0'=4,'ray_1'=8,'ray_2'=2,'row'=4] {'ray_0'}, dimensions={0}, use_global_device_ids=true | all-gather | bytes 327680 | tf_op jit(solution)/shard_map/all_gather | solution.py:41
  78.5 12.2 %all_gather.37 = f32[4,16,1024]{2,1,0:T(8,128)S(1)} all-gather(f32[1,16,1024]{2,1,0:T(8,128)S(1)} %get-tuple-element.25), channel_id=1, replica_groups=mesh['ray_0'=4,'ray_1'=8,'ray_2'=2,'row'=4] {'ray_0'}, dimensions={0}, use_global_device_ids=true | all-gather | bytes 327680 | tf_op jit(solution)/shard_map/all_gather | solution.py:41
  90.7 25.2 %all_gather.39 = f32[8,16,1024]{2,1,0:T(8,128)S(1)} all-gather(f32[1,16,1024]{2,1,0:T(8,128)S(1)} %get-tuple-element.26), channel_id=1, replica_groups=mesh['ray_0'=4,'ray_1'=8,'ray_2'=2,'row'=4] {'ray_1'}, dimensions={0}, use_global_device_ids=true | all-gather | bytes 589824 | tf_op jit(solution)/shard_map/all_gather | solution.py:41
  116.1 12.3 %all_gather.40 = f32[4,16,1024]{2,1,0:T(8,128)S(1)} all-gather(f32[1,16,1024]{2,1,0:T(8,128)S(1)} %get-tuple-element.5), channel_id=1, replica_groups=mesh['ray_0'=4,'ray_1'=8,'ray_2'=2,'row'=4] {'ray_0'}, dimensions={0}, use_global_device_ids=true | all-gather | bytes 327680 | tf_op jit(solution)/shard_map/all_gather | solution.py:41
  129.2 4.6 %multiply_subtract_fusion.2 = (f32[32,16,1024]{2,1,0:T(8,128)S(1)}, f32[32,16,1024]{2,1,0:T(8,128)S(1)}, f32[32,16,1024]{2,1,0:T(8,128)S(1)}) fusion(f32[]{:T(128)} %bitcast.10, f32[32,16,1024]{2,1,0:T(8,128)S(1)} %copy-done, f32[2,16,1024]{2,1,0:T(8,128)S(1)} %collective-permute-done.1, f32[2,16,1024]{2,1,0:T(8,128)S(1)} %collective-permute-done, ...), kind=kLoop, calls=%fused_computation.35 | loop fusion | flops 15728640 | bytes 17170444 | tf_op jit(solution)/shard_map/sub | solution.py:122
  134.0 3.5 %collective-permute-start.4 = (f32[32,1,1024]{2,1,0:T(1,128)S(1)}, f32[32,1,1024]{2,1,0:T(1,128)S(1)}, u32[]{:S(2)}, u32[]{:S(2)}) collective-permute-start(f32[32,1,1024]{2,1,0:T(1,128)S(1)} %get-tuple-element.19), channel_id=1, source_target_pairs={{0,1},{1,2},{2,3},{4,5},{5,6},{6,7},{8,9},{9,10},{10,11},{12,13},{... | collective-permute-start | bytes 393224 | tf_op jit(solution)/shard_map/ppermute | solution.py:21
  137.5 2.4 %collective-permute-start.5 = (f32[32,1,1024]{2,1,0:T(1,128)S(1)}, f32[32,1,1024]{2,1,0:T(1,128)S(1)}, u32[]{:S(2)}, u32[]{:S(2)}) collective-permute-start(f32[32,1,1024]{2,1,0:T(1,128)S(1)} %get-tuple-element.20), channel_id=1, source_target_pairs={{1,0},{2,1},{3,2},{5,4},{6,5},{7,6},{9,8},{10,9},{11,10},{13,12},{... | collective-permute-start | bytes 393224 | tf_op jit(solution)/shard_map/ppermute | solution.py:23
  140.8 3.5 %collective-permute-done.5 = f32[32,1,1024]{2,1,0:T(1,128)S(1)} collective-permute-done((f32[32,1,1024]{2,1,0:T(1,128)S(1)}, f32[32,1,1024]{2,1,0:T(1,128)S(1)}, u32[]{:S(2)}, u32[]{:S(2)}) %collective-permute-start.5) | collective-permute-done | bytes 131104 | tf_op jit(solution)/shard_map/ppermute | solution.py:23
  144.3 5.5 %fusion.4 = f32[32,16,1024]{2,1,0:T(8,128)} fusion(f32[32,16,1024]{2,1,0:T(8,128)S(1)} %get-tuple-element.15, f32[32,1,1024]{2,1,0:T(1,128)S(1)} %collective-permute-done.5, f32[32,16,1024]{2,1,0:T(8,128)S(1)} %get-tuple-element.16, f32[32,1,1024]{2,1,0:T(1,128)S(1)} %collective-permute-done.4, f32[1,16,1024]{2,1,0:T(8,128)S(1)} %fusion.51, ...), kind=kLoop, calls=%fused_computation.16 | loop fusion | flops 19398656 | bytes 19529728 | tf_op jit(solution)/shard_map/mul | solution.py:138
  (18 shorter events, 3.5 us)
Async XLA Ops:
  1.0 17.8 %collective-permute-start = (f32[2,16,1024]{2,1,0:T(8,128)S(1)}, f32[2,16,1024]{2,1,0:T(8,128)S(1)}, u32[]{:S(2)}, u32[]{:S(2)}) collective-permute-start(f32[2,16,1024]{2,1,0:T(8,128)S(1)} %get-tuple-element.22), channel_id=1, source_target_pairs={{4,0},{8,4},{12,8},{16,12},{20,16},{24,20},{28,24},{32,28},{36,32}... | collective-permute-start | bytes 393224 | tf_op jit(solution)/shard_map/ppermute | solution.py:23
  8.5 8.4 %collective-permute-start.1 = (f32[2,16,1024]{2,1,0:T(8,128)S(1)}, f32[2,16,1024]{2,1,0:T(8,128)S(1)}, u32[]{:S(2)}, u32[]{:S(2)}) collective-permute-start(f32[2,16,1024]{2,1,0:T(8,128)S(1)} %get-tuple-element.23), channel_id=1, source_target_pairs={{0,4},{4,8},{8,12},{12,16},{16,20},{20,24},{24,28},{28,32},{32,36}... | collective-permute-start | bytes 393224 | tf_op jit(solution)/shard_map/ppermute | solution.py:21
  16.9 13.2 %copy-start = (f32[32,16,1024]{2,1,0:T(8,128)S(1)}, f32[32,16,1024]{2,1,0:T(8,128)}, u32[]{:S(2)}) copy-start(f32[32,16,1024]{2,1,0:T(8,128)} %param.4) | copy-start | bytes 6291460
  19.1 8.6 %collective-permute-start.2 = (f32[36,2,1024]{2,1,0:T(2,128)S(1)}, f32[36,2,1024]{2,1,0:T(2,128)S(1)}, u32[]{:S(2)}, u32[]{:S(2)}) collective-permute-start(f32[36,2,1024]{2,1,0:T(2,128)S(1)} %get-tuple-element.17), channel_id=1, source_target_pairs={{1,0},{2,1},{3,2},{5,4},{6,5},{7,6},{9,8},{10,9},{11,10},{13,12},{... | collective-permute-start | bytes 884744 | tf_op jit(solution)/shard_map/ppermute | solution.py:23
  21.4 8.6 %collective-permute-start.3 = (f32[36,2,1024]{2,1,0:T(2,128)S(1)}, f32[36,2,1024]{2,1,0:T(2,128)S(1)}, u32[]{:S(2)}, u32[]{:S(2)}) collective-permute-start(f32[36,2,1024]{2,1,0:T(2,128)S(1)} %get-tuple-element.18), channel_id=1, source_target_pairs={{0,1},{1,2},{2,3},{4,5},{5,6},{6,7},{8,9},{9,10},{10,11},{12,13},{... | collective-permute-start | bytes 884744 | tf_op jit(solution)/shard_map/ppermute | solution.py:21
  134.0 6.9 %collective-permute-start.4 = (f32[32,1,1024]{2,1,0:T(1,128)S(1)}, f32[32,1,1024]{2,1,0:T(1,128)S(1)}, u32[]{:S(2)}, u32[]{:S(2)}) collective-permute-start(f32[32,1,1024]{2,1,0:T(1,128)S(1)} %get-tuple-element.19), channel_id=1, source_target_pairs={{0,1},{1,2},{2,3},{4,5},{5,6},{6,7},{8,9},{9,10},{10,11},{12,13},{... | collective-permute-start | bytes 393224 | tf_op jit(solution)/shard_map/ppermute | solution.py:21
  137.5 6.9 %collective-permute-start.5 = (f32[32,1,1024]{2,1,0:T(1,128)S(1)}, f32[32,1,1024]{2,1,0:T(1,128)S(1)}, u32[]{:S(2)}, u32[]{:S(2)}) collective-permute-start(f32[32,1,1024]{2,1,0:T(1,128)S(1)} %get-tuple-element.20), channel_id=1, source_target_pairs={{1,0},{2,1},{3,2},{5,4},{6,5},{7,6},{9,8},{10,9},{11,10},{13,12},{... | collective-permute-start | bytes 393224 | tf_op jit(solution)/shard_map/ppermute | solution.py:23
where the time goes:
time: 151 us; the launch traced here: 150 us
  blocking collectives  91.1 us (60%)
  starting transfers between devices  21.1 us (14%)
  other arithmetic  20.1 us (13%)
  waiting for transfers between devices  10.8 us (7%)
  local copies, waits for them, and re-layouts  4.77 us (3%)
  between operations  2.03 us (1%)
    all_gather x7, blocking collectives, prefix_by_axis(): pieces = jax.tree.map(lambda part: lax.all_gather(part, axis), subtotal)  91.1 us
    ppermute x3, starting transfers between devices, with_halo(): lax.ppermute(head, axis, [((i + 1) % count, i) for i in range(ends)])  12.2 us
    ppermute x3, starting transfers between devices, with_halo(): lax.ppermute(tail, axis, [(i, (i + 1) % count) for i in range(ends)])  8.89 us
    ppermute x3, waiting for transfers between devices, with_halo(): lax.ppermute(head, axis, [((i + 1) % count, i) for i in range(ends)])  6.22 us
    mul x1, other arithmetic, local(): return adj_density * float(full_depth)  5.52 us
    another operation x1, other arithmetic, local(): local_trans = jnp.exp(-(jnp.cumsum(optical, axis=0) - optical))  5.24 us
    ppermute x3, waiting for transfers between devices, with_halo(): lax.ppermute(tail, axis, [(i, (i + 1) % count) for i in range(ends)])  4.57 us
    sub x1, other arithmetic, local(): adj_x = scaled * light_dir[0] - bent * grad_x  4.57 us
  transfers between devices with their start and end apart: 6, of which 4 were waited for; matrix products, arithmetic and copies ran while one was open for 4% of the time, Pallas kernels for 0%

commit v1 on v0

v1 whole, which is shorter than its diff:
```python
import functools

import jax
import jax.numpy as jnp
from jax import lax
from jax.experimental import pallas as pl
from jax.experimental.pallas import tpu as pltpu
from jax.sharding import Mesh
from jax.sharding import PartitionSpec as P

RAY = ("ray_0", "ray_1", "ray_2")
EXTINCTION = 0.7
LANES = 128
BLOCK = 8
VM = pl.BlockSpec(memory_space=pltpu.VMEM)
SM = pl.BlockSpec(memory_space=pltpu.SMEM)
HBM = pl.BlockSpec(memory_space=pltpu.HBM)


def sds(*shape):
    return jax.ShapeDtypeStruct(shape, jnp.float32)


def col(c):
    return pl.ds(c * LANES, LANES)


def half(h):
    return pl.ds(h * 8, 8)


def ids():
    lane = lax.broadcasted_iota(jnp.int32, (8, LANES), 1)
    sub = lax.broadcasted_iota(jnp.int32, (8, LANES), 0)
    return lane == 0, lane == LANES - 1, sub == 0, sub == 7


def wide(row):
    return jnp.broadcast_to(row, (8, LANES))


def col_neighbours(tiles, first, last):
    right = [pltpu.roll(t, 1, 1) for t in tiles]
    left = [pltpu.roll(t, LANES - 1, 1) for t in tiles]
    zero = jnp.zeros((8, LANES), jnp.float32)
    n = len(tiles)
    before = [jnp.where(first, right[c - 1] if c else zero, right[c]) for c in range(n)]
    after = [jnp.where(last, left[c + 1] if c < n - 1 else zero, left[c]) for c in range(n)]
    return before, after


def row_neighbours(top, bottom, above, below, first, last):
    down = [pltpu.roll(t, 1, 0) for t in (top, bottom)]
    up = [pltpu.roll(t, 7, 0) for t in (top, bottom)]
    before = (jnp.where(first, above, down[0]), jnp.where(first, down[0], down[1]))
    after = (jnp.where(last, up[1], up[0]), jnp.where(last, below, up[1]))
    return before, after


def absorbed(optical, terms):
    value = 1.0 - optical * (1.0 / terms)
    for n in range(terms - 1, 1, -1):
        value = 1.0 - optical * (1.0 / n) * value
    return optical * value


def gather_kernel(
    place, tint, dens, cot, held, row_first, row_last, to_near, to_cross, rho, held_cot, sems, cot_sem
):
    ndep, nrow, _ = dens.shape
    core_first = place[0] == 0
    colours = pltpu.make_async_copy(cot, held_cot, cot_sem)
    copies = []
    for b in range(ndep // BLOCK):
        part = pl.ds(b * BLOCK, BLOCK)
        copies.append(pltpu.make_async_copy(dens.at[part], held.at[part], sems.at[b]))
        copies[-1].start()
    colours.start()
    for b, copy in enumerate(copies):
        copy.wait()
        for k in range(b * BLOCK, (b + 1) * BLOCK):
            row_first[k] = held[k, 0:1, :]
            row_last[k] = held[k, nrow - 1 : nrow, :]
    first_layer, last_layer = held[0], held[ndep - 1]
    to_near[...] = jnp.where(core_first, last_layer, first_layer)
    to_cross[...] = jnp.where(core_first, first_layer, last_layer)
    colours.wait()
    rho[...] = held_cot[0] * tint[0] + held_cot[1] * tint[1] + held_cot[2] * tint[2]


def shade(light, mid, before, after, lows, highs, masks):
    lx, ly, lz = light
    first, last, head, tail = masks
    nc = len(mid[0])
    zs = [col_neighbours(mid[h], first, last) for h in range(2)]
    out = [[None] * nc, [None] * nc]
    for c in range(nc):
        ys = row_neighbours(mid[0][c], mid[1][c], lows(c), highs(c), head, tail)
        for h in range(2):
            dx = after(h, c) - before(h, c)
            dy = ys[1][h] - ys[0][h]
            dz = zs[h][1][c] - zs[h][0][c]
            inv = lax.rsqrt(4.0 + dx * dx + dy * dy + dz * dz)
            out[h][c] = dx, dy, dz, inv, (lx * dx + ly * dy + lz * dz) * inv
    return out


def opacity(d, step):
    return d * (step - d * (step**2 / 2 - d * (step**3 / 6)))


def forward_kernel(
    step, place, light, dens, near, cross, low, high, rho,
    packed, ends, trans,
):
    ndep, _, ncol = dens.shape
    nc = ncol // LANES
    lights = light[0], light[1], light[2]
    masks = ids()
    core_first = place[0] == 0
    for c in range(nc):
        for h in range(2):
            trans[half(h), col(c)] = jnp.ones((8, LANES), jnp.float32)
            ends[1, half(h), col(c)] = jnp.zeros((8, LANES), jnp.float32)

    def outer(h, c, lower):
        a, b = near[half(h), col(c)], cross[half(h), col(c)]
        return jnp.where(core_first, b, a) if lower else jnp.where(core_first, a, b)

    def layer(k, before, after):
        mid = [[dens[k, half(h), col(c)] for c in range(nc)] for h in range(2)]
        tiles = shade(
            lights, mid, before, after,
            lambda c: wide(low[k, :, col(c)]), lambda c: wide(high[k, :, col(c)]), masks,
        )
        for c in range(nc):
            for h in range(2):
                d, q = mid[h][c], tiles[h][c][4]
                t = trans[half(h), col(c)]
                w = t * opacity(d, step)
                trans[half(h), col(c)] = t - w
                ends[1, half(h), col(c)] += w * d * (0.5 + 0.5 * q)

    layer(0, lambda h, c: outer(h, c, True), lambda h, c: dens[1, half(h), col(c)])

    @pl.loop(1, ndep - 1)
    def _(k):
        layer(k, lambda h, c: dens[k - 1, half(h), col(c)], lambda h, c: dens[k + 1, half(h), col(c)])

    layer(ndep - 1, lambda h, c: dens[ndep - 2, half(h), col(c)], lambda h, c: outer(h, c, False))

    for c in range(nc):
        for h in range(2):
            ends[0, half(h), col(c)] = trans[half(h), col(c)]
    rims = []
    for rim in (low, high):
        total = rim[0]
        for k in range(1, ndep):
            total = total + rim[k]
        rims.append(1.0 - absorbed(total * step, 7))
    for c in range(nc):
        cs = slice(c * LANES, (c + 1) * LANES)
        for h in range(2):
            t = trans[half(h), col(c)]
            v = ends[1, half(h), col(c)] * rho[half(h), col(c)]
            for b in range(4):
                a = h * 4 + b
                p = a * nc + c
                packed[p, :, 0:128] = t[2 * b : 2 * b + 1]
                packed[p, :, 128:256] = t[2 * b + 1 : 2 * b + 2]
                packed[p, :, 256:384] = rims[0][:, cs] if a < 4 else rims[1][:, cs]
                packed[p, :, 384:512] = v[2 * b : 2 * b + 1]
                packed[p, :, 512:640] = v[2 * b + 1 : 2 * b + 2]


def adjoint_kernel(
    step, depth, place, light, dens, near, cross, low, high, rho, ends,
    part, adj_y, adj_z, to_near, to_cross, y_first, y_last,
    held, xs, parts, ys, zs, trans, colour, in_sems, part_sems, y_sems, z_sems,
):
    ndep, _, ncol = dens.shape
    nc = ncol // LANES
    lx, ly, lz = lights = light[0], light[1], light[2]
    masks = ids()
    core_first = place[0] == 0
    blocks = ndep // BLOCK
    arrivals = []
    for b in range(blocks):
        at = pl.ds(b * BLOCK, BLOCK)
        arrivals.append(
            pltpu.make_async_copy(dens.at[at], held.at[pl.ds(b * BLOCK + 1, BLOCK)], in_sems.at[b])
        )
        arrivals[-1].start()
    for c in range(nc):
        for h in range(2):
            at = (half(h), col(c))
            a, b = near[at], cross[at]
            held[0, half(h), col(c)] = jnp.where(core_first, b, a)
            held[ndep + 1, half(h), col(c)] = jnp.where(core_first, a, b)
            trans[at] = jnp.ones((8, LANES), jnp.float32)
            colour[at] = jnp.zeros((8, LANES), jnp.float32)
            for k in (0, 1):
                xs[k, half(h), col(c)] = jnp.zeros((8, LANES), jnp.float32)
            parts[0, half(h), col(c)] = jnp.zeros((8, LANES), jnp.float32)

    def layer(k):
        mid = [[held[k + 1, half(h), col(c)] for c in range(nc)] for h in range(2)]
        tiles = shade(
            lights, mid,
            lambda h, c: held[k, half(h), col(c)], lambda h, c: held[k + 2, half(h), col(c)],
            lambda c: wide(low[k, :, col(c)]), lambda c: wide(high[k, :, col(c)]), masks,
        )
        for c in range(nc):
            for h in range(2):
                at = (half(h), col(c))
                d = mid[h][c]
                dx, dy, dz, inv, q = tiles[h][c]
                lit = 0.5 + 0.5 * q
                t = trans[at]
                w = t * opacity(d, step)
                t = t - w
                trans[at] = t
                wd = w * d
                e = colour[at] + wd * lit
                colour[at] = e
                r = rho[at] * depth
                glow = r * (w * lit + step * (t * (d * lit) + e))
                s = wd * inv * (0.5 * r)
                m = q * inv
                x = s * (lx - m * dx)
                y = s * (ly - m * dy)
                xs[k + 2, half(h), col(c)] = x
                ys[k, half(h), col(c)] = y
                zs[k, half(h), col(c)] = s * (lz - m * dz)
                parts[k + 1, half(h), col(c)] = glow
                parts[k, half(h), col(c)] += xs[k, half(h), col(c)] - x
                if h == 0:
                    y_first[k, :, col(c)] = y[0:1]
                else:
                    y_last[k, :, col(c)] = y[7:8]

    copies = []

    def send(source, target, start, shift, count, sem):
        copies.append(
            pltpu.make_async_copy(
                source.at[pl.ds(start + shift, count)], target.at[pl.ds(start, count)], sem
            )
        )
        copies[-1].start()

    arrivals[0].wait()
    for b in range(blocks):
        if b < blocks - 1:
            arrivals[b + 1].wait()
        pl.loop(b * BLOCK, (b + 1) * BLOCK)(layer)
        send(ys, adj_y, b * BLOCK, 0, BLOCK, y_sems.at[b])
        send(zs, adj_z, b * BLOCK, 0, BLOCK, z_sems.at[b])
        start = max(b * BLOCK - 1, 0)
        send(parts, part, start, 1, (b + 1) * BLOCK - 1 - start, part_sems.at[b])
    for c in range(nc):
        for h in range(2):
            at = (half(h), col(c))
            parts[ndep, half(h), col(c)] += xs[ndep, half(h), col(c)]
            first_x = xs[2, half(h), col(c)]
            last_x = xs[ndep + 1, half(h), col(c)] / ends[0, half(h), col(c)]
            to_near[at] = jnp.where(core_first, last_x, first_x)
            to_cross[at] = jnp.where(core_first, first_x, last_x)
    send(parts, part, ndep - 1, 1, 1, part_sems.at[blocks])
    for copy in copies:
        copy.wait()


def scan_kernel(packed, out):
    slabs = packed.shape[0]
    front = jnp.ones((1, 384), jnp.float32)
    for m in range(slabs):
        out[m, :, 0:384] = front
        if m < slabs - 1:
            front = front * packed[m, :, 0:384]
    behind = jnp.zeros((1, 256), jnp.float32)
    for m in reversed(range(slabs)):
        out[m, :, 384:640] = behind
        if m:
            behind = behind + out[m, :, 0:256] * packed[m, :, 384:640]


def combine_kernel(
    step, depth, place, scanned, x_near, x_cross, y_low, y_high, rho, ends, part, adj_y, adj_z,
    out, front, base, edge, parts, ys, zs, part_sems, y_sems, z_sems, out_sems,
):
    ndep, _, ncol = part.shape
    nc = ncol // LANES
    first, last, head, tail = ids()
    core_first = place[0] == 0
    blocks = ndep // BLOCK
    arrivals = []
    for b in range(blocks):
        at = pl.ds(b * BLOCK, BLOCK)
        arrivals.append(
            [
                pltpu.make_async_copy(source.at[at], target.at[at], sems.at[b])
                for source, target, sems in ((part, parts, part_sems), (adj_y, ys, y_sems), (adj_z, zs, z_sems))
            ]
        )
        for copy in arrivals[-1]:
            copy.start()
    for c in range(nc):
        for a in range(8):
            p = a * nc + c
            front[2 * a : 2 * a + 1, col(c)] = scanned[p, :, 0:128]
            front[2 * a + 1 : 2 * a + 2, col(c)] = scanned[p, :, 128:256]
            base[2 * a : 2 * a + 1, col(c)] = scanned[p, :, 384:512]
            base[2 * a + 1 : 2 * a + 2, col(c)] = scanned[p, :, 512:640]
        edge[0, :, col(c)] = scanned[c, :, 256:384]
        edge[1, :, col(c)] = scanned[7 * nc + c, :, 256:384]
    for c in range(nc):
        for h in range(2):
            at = (half(h), col(c))
            base[at] = (depth * step) * (base[at] + front[at] * (rho[at] * ends[1, half(h), col(c)]))

    def outer(h, c, lower):
        a, b = x_near[half(h), col(c)], x_cross[half(h), col(c)]
        if lower:
            return jnp.where(core_first, b, a)
        return jnp.where(core_first, a, b) * -ends[0, half(h), col(c)]

    def layer(k, extra=None):
        zt, yt = [[], []], [[], []]
        for h in range(2):
            for c in range(nc):
                f = front[half(h), col(c)]
                zt[h].append(f * zs[k, half(h), col(c)])
                yt[h].append(f * ys[k, half(h), col(c)])
        zn = [col_neighbours(zt[h], first, last) for h in range(2)]
        for c in range(nc):
            lo = wide(edge[0, :, col(c)] * y_low[k, :, col(c)])
            hi = wide(edge[1, :, col(c)] * y_high[k, :, col(c)])
            yn = row_neighbours(yt[0][c], yt[1][c], lo, hi, head, tail)
            for h in range(2):
                at, cell = (half(h), col(c)), (k, half(h), col(c))
                own = parts[cell]
                if extra is not None:
                    own = own + outer(h, c, extra)
                parts[cell] = (front[at] * own - base[at]) + (
                    (yn[0][h] - yn[1][h]) + (zn[h][0][c] - zn[h][1][c])
                )

    copies = []
    for b in range(blocks):
        start, stop = b * BLOCK, (b + 1) * BLOCK
        for copy in arrivals[b]:
            copy.wait()
        if b == 0:
            layer(0, True)
            start = 1
        if stop == ndep:
            stop = ndep - 1
        pl.loop(start, stop)(layer)
        if stop == ndep - 1:
            layer(stop, False)
        at = pl.ds(b * BLOCK, BLOCK)
        copies.append(pltpu.make_async_copy(parts.at[at], out.at[at], out_sems.at[b]))
        copies[-1].start()
    for copy in copies:
        copy.wait()


def params(mib):
    return pltpu.CompilerParams(vmem_limit_bytes=mib << 20)


def cost(flops, nbytes):
    return pl.CostEstimate(flops=flops, bytes_accessed=nbytes, transcendentals=0)


def near_memory(*arrays):
    return [pltpu.with_memory_space_constraint(a, pltpu.VMEM) for a in arrays]


def far_memory(*arrays):
    return [pltpu.with_memory_space_constraint(a, pltpu.HBM) for a in arrays]


def local(density, light_dir, colour_tint, cotangent):
    ndep, nrow, ncol = density.shape
    slabs = lax.axis_size(RAY)
    rows = lax.axis_size("row")
    full_depth = float(ndep * slabs)
    step = EXTINCTION / full_depth
    place = lax.axis_index(RAY[2]).reshape(1).astype(jnp.int32)
    swap = [(0, 1), (1, 0)]
    cross = [(i, i + 1) for i in range(1, slabs - 1, 2)] + [(i + 1, i) for i in range(1, slabs - 1, 2)]
    upward = [(i, i + 1) for i in range(rows - 1)]
    downward = [(i + 1, i) for i in range(rows - 1)]

    def exchange(row_first, row_last, to_near, to_cross):
        return near_memory(
            lax.ppermute(to_near, RAY[2], swap),
            lax.ppermute(to_cross, RAY, cross),
            lax.ppermute(row_last, "row", upward),
            lax.ppermute(row_first, "row", downward),
        )

    def vmem(*shape):
        return pltpu.VMEM(shape, jnp.float32)

    def hbm(*shape):
        return pltpu.HBM(shape, jnp.float32)

    cube, layer, rim = (ndep, nrow, ncol), (nrow, ncol), (ndep, 1, ncol)
    share = (slabs, 1, 5 * LANES)
    blocks = ndep // BLOCK
    cells = ndep * nrow * ncol
    sem = pltpu.SemaphoreType.DMA
    held, row_first, row_last, to_near, to_cross, rho = pl.pallas_call(
        gather_kernel,
        out_shape=(vmem(*cube), vmem(*rim), vmem(*rim), vmem(*layer), vmem(*layer), vmem(*layer)),
        in_specs=[SM, SM, HBM, HBM],
        out_specs=[VM] * 6,
        scratch_shapes=[vmem(*cotangent.shape), sem((blocks,)), sem],
        compiler_params=params(4),
        name="gather",
    )(place, colour_tint, *far_memory(density, cotangent))
    halos = exchange(row_first, row_last, to_near, to_cross)
    packed, ends = pl.pallas_call(
        functools.partial(forward_kernel, step),
        out_shape=(vmem(*share), vmem(2, *layer)),
        in_specs=[SM, SM] + [VM] * 6,
        out_specs=[VM] * 2,
        scratch_shapes=[vmem(*layer)],
        compiler_params=params(4),
        cost_estimate=cost(50 * cells, 4 * cells),
        name="forward",
    )(place, light_dir, held, *halos, rho)

    scanned = lax.all_to_all(packed, RAY, 0, 0)
    part, adj_y, adj_z, to_near, to_cross, y_first, y_last = pl.pallas_call(
        functools.partial(adjoint_kernel, step, full_depth),
        out_shape=(hbm(*cube),) * 3 + (vmem(*layer), vmem(*layer), vmem(*rim), vmem(*rim)),
        in_specs=[SM, SM, HBM] + [VM] * 6,
        out_specs=[HBM] * 3 + [VM] * 4,
        scratch_shapes=[
            vmem(ndep + 2, nrow, ncol),
            vmem(ndep + 2, nrow, ncol),
            vmem(ndep + 1, nrow, ncol),
            vmem(*cube),
            vmem(*cube),
            vmem(*layer),
            vmem(*layer),
            sem((blocks,)),
            sem((blocks + 1,)),
            sem((blocks,)),
            sem((blocks,)),
        ],
        compiler_params=params(16),
        cost_estimate=cost(70 * cells, 16 * cells),
        name="adjoint",
    )(place, light_dir, *far_memory(density), *halos, rho, ends)
    scanned, to_near, to_cross, y_first, y_last = lax.optimization_barrier(
        (scanned, to_near, to_cross, y_first, y_last)
    )
    scanned = pl.pallas_call(
        scan_kernel,
        out_shape=vmem(*share),
        in_specs=[VM],
        out_specs=VM,
        compiler_params=params(4),
        name="scan",
    )(*near_memory(scanned))
    scanned = lax.all_to_all(scanned, RAY, 0, 0)
    rims = exchange(y_first, y_last, to_near, to_cross)
    return pl.pallas_call(
        functools.partial(combine_kernel, step, full_depth),
        out_shape=sds(*cube),
        in_specs=[SM] + [VM] * 7 + [HBM] * 3,
        out_specs=HBM,
        scratch_shapes=[
            vmem(*layer),
            vmem(*layer),
            vmem(2, 1, ncol),
            vmem(*cube),
            vmem(*cube),
            vmem(*cube),
            sem((blocks,)),
            sem((blocks,)),
            sem((blocks,)),
            sem((blocks,)),
        ],
        compiler_params=params(16),
        cost_estimate=cost(12 * cells, 16 * cells),
        name="combine",
    )(place, *near_memory(scanned), *rims, rho, ends, *far_memory(part, adj_y, adj_z))


def solution(mesh):
    torus = Mesh(
        mesh.devices.reshape(4, 8, 2, mesh.shape["row"]), ("ray_0", "ray_1", "ray_2", "row")
    )
    placed = (P(RAY, "row", None), P(), P(), P(None, "row", None))
    return jax.shard_map(
        local, mesh=torus, in_specs=placed, out_specs=P(RAY, "row", None), check_vma=False
    )
```

time: 151 us -> 72.3 us (0.48)
  blocking collectives: 91.1 us -> 0 us
  Pallas kernels: 0 us -> 22.2 us
  starting transfers between devices: 21.1 us -> 43 us
  other arithmetic: 20.1 us -> 0 us
  waiting for transfers between devices: 10.8 us -> 5.87 us
  local copies, waits for them, and re-layouts: 4.77 us -> 0.67 us
  between operations: 2.03 us -> 0.13 us
    all_gather x7 -> x0, blocking collectives: 91.1 us -> none  [prefix_by_axis(): pieces = jax.tree.map(lambda part: lax.all_gather(part, axis), subtotal)]
    pallas_call x0 -> x5, Pallas kernels: none -> 22.2 us  [the longest x1 8.32 us: local(): pl.pallas_call(functools.partial(adjoint_kernel, step, full_depth), out_s...]
    all_to_all x0 -> x2, starting transfers between devices: none -> 18 us  [the longest x1 9.13 us: local(): scanned = lax.all_to_all(scanned, RAY, 0, 0)]
    another operation x2 -> x0, other arithmetic: 6.97 us -> none  [the longest x1 5.24 us: local(): local_trans = jnp.exp(-(jnp.cumsum(optical, axis=0) - optical))]
    ppermute x6 -> x8, waiting for transfers between devices: 10.8 us -> 4.67 us  [the longest x2 4.65 us: exchange(): lax.ppermute(to_cross, RAY, cross)]
    mul x2 -> x0, other arithmetic: 5.53 us -> none  [the longest x1 5.52 us: local(): return adj_density * float(full_depth)]
    sub x1 -> x0, other arithmetic: 4.57 us -> none  [local(): adj_x = scaled * light_dir[0] - bent * grad_x]
    ppermute x6 -> x8, starting transfers between devices: 21.1 us -> 24.9 us  [the longest x2 13.1 us: exchange(): lax.ppermute(to_cross, RAY, cross)]
  transfers between devices with their start and end apart: 6 -> 10, of which waited for: 4 -> 3; matrix products, arithmetic and copies ran while one was open for 4% -> 0% of each run, Pallas kernels for 0% -> 12%
where the time goes in v1:
time: 72.3 us; the launch traced here: 71.9 us
  starting transfers between devices  43 us (59%)
  Pallas kernels  22.2 us (31%)
  waiting for transfers between devices  5.87 us (8%)
    ppermute x2, starting transfers between devices, exchange(): lax.ppermute(to_cross, RAY, cross)  13.1 us
    all_to_all x1, starting transfers between devices, local(): scanned = lax.all_to_all(scanned, RAY, 0, 0)  9.13 us
    all_to_all x1, starting transfers between devices, local(): scanned = lax.all_to_all(packed, RAY, 0, 0)  8.9 us
    pallas_call x1, Pallas kernels, local(): pl.pallas_call(functools.partial(adjoint_kernel, step, full_depth), out_s...  8.32 us
    ppermute x2, starting transfers between devices, exchange(): lax.ppermute(row_last, 'row', upward)  6.97 us
    pallas_call x1, Pallas kernels, local(): pl.pallas_call(functools.partial(combine_kernel, step, full_depth), out_s...  5.91 us
    pallas_call x1, Pallas kernels, local(): pl.pallas_call(functools.partial(forward_kernel, step), out_shape=(vmem(*...  5.04 us
    ppermute x2, starting transfers between devices, exchange(): lax.ppermute(row_first, 'row', downward)  4.73 us
  transfers between devices with their start and end apart: 10, of which 3 were waited for; matrix products, arithmetic and copies ran while one was open for 0% of the time, Pallas kernels for 12%

profile of v1, /device:TPU:14, one launch (start us, length us, event | category | flops | bytes accessed | tf_op | source)
XLA Modules:
  0.0 71.9 jit_solution(6480687286595129429)
XLA Ops:
  0.0 0.7 copy-done.1
  0.7 2.2 %gather.1 = (f32[32,16,1024]{2,1,0:T(8,128)S(1)}, f32[32,1,1024]{2,1,0:T(1,128)S(1)}, f32[32,1,1024]{2,1,0:T(1,128)S(1)}, f32[16,1024]{1,0:T(8,128)S(1)}, f32[16...) custom-call(s32[1]{0:T(128)} %bitcast.place, f32[3]{0:T(128)S(1)} %copy-done.1, f32[32,16,1024]{2,1,0:T(8,128)} %dens.3, ...), custom_call_target="tpu_custom_call" | custom-call | tf_op jit(solution)/shard_map/gather/pallas_call | solution.py:416
  2.8 3.5 %collective-permute-start.2 = (f32[32,1,1024]{2,1,0:T(1,128)S(1)}, f32[32,1,1024]{2,1,0:T(1,128)S(1)}, u32[]{:S(2)}, u32[]{:S(2)}) collective-permute-start(f32[32,1,1024]{2,1,0:T(1,128)S(1)} %get-tuple-element.28), channel_id=1, source_target_pairs={{0,1},{1,2},{2,3},{4,5},{5,6},{6,7},{8,9},{9,10},{10,11},{12,13},{... | collective-permute-start | bytes 393224 | tf_op jit(solution)/shard_map/ppermute | solution.py:401
  6.3 2.4 %collective-permute-start.3 = (f32[32,1,1024]{2,1,0:T(1,128)S(1)}, f32[32,1,1024]{2,1,0:T(1,128)S(1)}, u32[]{:S(2)}, u32[]{:S(2)}) collective-permute-start(f32[32,1,1024]{2,1,0:T(1,128)S(1)} %get-tuple-element.29), channel_id=1, source_target_pairs={{1,0},{2,1},{3,2},{5,4},{6,5},{7,6},{9,8},{10,9},{11,10},{13,12},{... | collective-permute-start | bytes 393224 | tf_op jit(solution)/shard_map/ppermute | solution.py:402
  8.7 0.1 collective-permute-start
  8.8 8.1 %collective-permute-start.1 = (f32[16,1024]{1,0:T(8,128)S(1)}, f32[16,1024]{1,0:T(8,128)S(1)}, u32[]{:S(2)}, u32[]{:S(2)}) collective-permute-start(f32[16,1024]{1,0:T(8,128)S(1)} %get-tuple-element.27), channel_id=1, source_target_pairs={{4,8},{12,16},{20,24},{28,32},{36,40},{44,48},{52,56},{60,64},{68,... | collective-permute-start | bytes 196616 | tf_op jit(solution)/shard_map/ppermute | solution.py:400
  16.9 0.0 collective-permute-done.near
  16.9 1.9 %collective-permute-done.1.cross = f32[16,1024]{1,0:T(8,128)S(1)} collective-permute-done((f32[16,1024]{1,0:T(8,128)S(1)}, f32[16,1024]{1,0:T(8,128)S(1)}, u32[]{:S(2)}, u32[]{:S(2)}) %collective-permute-start.1) | collective-permute-done | bytes 65568 | tf_op jit(solution)/shard_map/ppermute | solution.py:400
  18.9 0.0 collective-permute-done.2.low
  18.9 0.0 collective-permute-done.3.high
  18.9 5.0 %forward.1 = (f32[64,1,640]{2,1,0:T(1,128)}, f32[2,16,1024]{2,1,0:T(8,128)S(1)}) custom-call(s32[1]{0:T(128)} %bitcast.place, f32[3]{0:T(128)S(1)} %copy-done, f32[32,16,1024]{2,1,0:T(8,128)S(1)} %get-tuple-element.25.dens, f32[16,1024]{1,0:T(8,128)S(1)} %collective-permute-done.near, f32[16,1024]{1,0:T(8,128)S(1)} %collective-permute-done.1.cross, ...), custom_call_target="tpu_custom_call" | custom-call | flops 26214400 | bytes 2097152 | tf_op jit(solution)/shard_map/forward/pallas_call | solution.py:426
  23.9 8.9 %all-to-all-start = ((f32[64,1,640]{2,1,0:T(1,128)}), f32[64,1,640]{2,1,0:T(1,128)S(1)}, u32[]{:S(2)}, u32[]{:S(2)}) async-start(f32[64,1,640]{2,1,0:T(1,128)} %get-tuple-element.31), calls=%async_computation | async-start | bytes 327680 | tf_op jit(solution)/shard_map/all_to_all | solution.py:437
  32.8 8.3 %adjoint.1 = (f32[32,16,1024]{2,1,0:T(8,128)}, f32[32,16,1024]{2,1,0:T(8,128)}, f32[32,16,1024]{2,1,0:T(8,128)}, f32[16,1024]{1,0:T(8,128)S(1)}, f32[16,1024]{1,...) custom-call(s32[1]{0:T(128)} %bitcast.place, f32[3]{0:T(128)S(1)} %copy-done, ...), custom_call_target="tpu_custom_call" | custom-call | flops 36700160 | bytes 8388608 | tf_op jit(solution)/shard_map/adjoint/pallas_call | solution.py:438
  41.2 1.2 %all-to-all-done.packed = f32[64,1,640]{2,1,0:T(1,128)S(1)} async-done(((f32[64,1,640]{2,1,0:T(1,128)}), f32[64,1,640]{2,1,0:T(1,128)S(1)}, u32[]{:S(2)}, u32[]{:S(2)}) %all-to-all-start) | async-done | bytes 163872 | tf_op jit(solution)/shard_map/all_to_all | solution.py:437
  42.4 0.8 %scan.1 = f32[64,1,640]{2,1,0:T(1,128)} custom-call(f32[64,1,640]{2,1,0:T(1,128)S(1)} %all-to-all-done.packed), custom_call_target="tpu_custom_call" | custom-call | tf_op jit(solution)/shard_map/scan/pallas_call | solution.py:463
  43.2 9.1 %all-to-all-start.1 = ((f32[64,1,640]{2,1,0:T(1,128)}), f32[64,1,640]{2,1,0:T(1,128)S(1)}, u32[]{:S(2)}, u32[]{:S(2)}) async-start(f32[64,1,640]{2,1,0:T(1,128)} %scan.1), calls=%async_computation.1 | async-start | bytes 327680 | tf_op jit(solution)/shard_map/all_to_all | solution.py:471
  52.3 3.5 %collective-permute-start.6 = (f32[32,1,1024]{2,1,0:T(1,128)S(1)}, f32[32,1,1024]{2,1,0:T(1,128)S(1)}, u32[]{:S(2)}, u32[]{:S(2)}) collective-permute-start(f32[32,1,1024]{2,1,0:T(1,128)S(1)} %get-tuple-element.40), channel_id=1, source_target_pairs={{0,1},{1,2},{2,3},{4,5},{5,6},{6,7},{8,9},{9,10},{10,11},{12,13},{... | collective-permute-start | bytes 393224 | tf_op jit(solution)/shard_map/ppermute | solution.py:401
  55.8 2.4 %collective-permute-start.7 = (f32[32,1,1024]{2,1,0:T(1,128)S(1)}, f32[32,1,1024]{2,1,0:T(1,128)S(1)}, u32[]{:S(2)}, u32[]{:S(2)}) collective-permute-start(f32[32,1,1024]{2,1,0:T(1,128)S(1)} %get-tuple-element.41), channel_id=1, source_target_pairs={{1,0},{2,1},{3,2},{5,4},{6,5},{7,6},{9,8},{10,9},{11,10},{13,12},{... | collective-permute-start | bytes 393224 | tf_op jit(solution)/shard_map/ppermute | solution.py:402
  58.2 0.1 collective-permute-start.4
  58.3 5.0 %collective-permute-start.5 = (f32[16,1024]{1,0:T(8,128)S(1)}, f32[16,1024]{1,0:T(8,128)S(1)}, u32[]{:S(2)}, u32[]{:S(2)}) collective-permute-start(f32[16,1024]{1,0:T(8,128)S(1)} %get-tuple-element.39), channel_id=1, source_target_pairs={{4,8},{12,16},{20,24},{28,32},{36,40},{44,48},{52,56},{60,64},{68,... | collective-permute-start | bytes 196616 | tf_op jit(solution)/shard_map/ppermute | solution.py:400
  63.2 0.0 collective-permute-done.4.x_near
  63.2 2.7 %collective-permute-done.5.x_cross = f32[16,1024]{1,0:T(8,128)S(1)} collective-permute-done((f32[16,1024]{1,0:T(8,128)S(1)}, f32[16,1024]{1,0:T(8,128)S(1)}, u32[]{:S(2)}, u32[]{:S(2)}) %collective-permute-start.5) | collective-permute-done | bytes 65568 | tf_op jit(solution)/shard_map/ppermute | solution.py:400
  66.0 0.0 collective-permute-done.6.y_low
  66.0 5.9 %combine.1 = f32[32,16,1024]{2,1,0:T(8,128)} custom-call(s32[1]{0:T(128)} %bitcast.place, f32[64,1,640]{2,1,0:T(1,128)S(1)} %all-to-all-done.1.scanned, f32[16,1024]{1,0:T(8,128)S(1)} %collective-permute-done.4.x_near, f32[16,1024]{1,0:T(8,128)S(1)} %collective-permute-done.5.x_cross, f32[32,1,1024]{2,1,0:T(1,128)S(1)} %collective-permute-done.6.y_low, ...), custom_call_target="tpu_custom_call" | custom-call | flops 6291456 | bytes 8388608 | tf_op jit(solution)/shard_map/combine/pallas_call | solution.py:473
  (5 shorter events, 0.0 us)
Async XLA Ops:
  0.0 18.9 %copy-start = (f32[3]{0:T(128)S(1)}, f32[3]{0:T(128)}, u32[]{:S(2)}) copy-start(f32[3]{0:T(128)} %light.3) | copy-start | bytes 40
  0.0 0.7 copy-start.1
  2.8 16.0 %collective-permute-start.2 = (f32[32,1,1024]{2,1,0:T(1,128)S(1)}, f32[32,1,1024]{2,1,0:T(1,128)S(1)}, u32[]{:S(2)}, u32[]{:S(2)}) collective-permute-start(f32[32,1,1024]{2,1,0:T(1,128)S(1)} %get-tuple-element.28), channel_id=1, source_target_pairs={{0,1},{1,2},{2,3},{4,5},{5,6},{6,7},{8,9},{9,10},{10,11},{12,13},{... | collective-permute-start | bytes 393224 | tf_op jit(solution)/shard_map/ppermute | solution.py:401
  6.3 12.5 %collective-permute-start.3 = (f32[32,1,1024]{2,1,0:T(1,128)S(1)}, f32[32,1,1024]{2,1,0:T(1,128)S(1)}, u32[]{:S(2)}, u32[]{:S(2)}) collective-permute-start(f32[32,1,1024]{2,1,0:T(1,128)S(1)} %get-tuple-element.29), channel_id=1, source_target_pairs={{1,0},{2,1},{3,2},{5,4},{6,5},{7,6},{9,8},{10,9},{11,10},{13,12},{... | collective-permute-start | bytes 393224 | tf_op jit(solution)/shard_map/ppermute | solution.py:402
  8.7 8.2 %collective-permute-start = (f32[16,1024]{1,0:T(8,128)S(1)}, f32[16,1024]{1,0:T(8,128)S(1)}, u32[]{:S(2)}, u32[]{:S(2)}) collective-permute-start(f32[16,1024]{1,0:T(8,128)S(1)} %get-tuple-element.26), channel_id=1, source_target_pairs={{0,4},{4,0},{1,5},{5,1},{2,6},{6,2},{3,7},{7,3},{8,12},{12,8},{9,1... | collective-permute-start | bytes 196616 | tf_op jit(solution)/shard_map/ppermute | solution.py:399
  8.8 10.1 %collective-permute-start.1 = (f32[16,1024]{1,0:T(8,128)S(1)}, f32[16,1024]{1,0:T(8,128)S(1)}, u32[]{:S(2)}, u32[]{:S(2)}) collective-permute-start(f32[16,1024]{1,0:T(8,128)S(1)} %get-tuple-element.27), channel_id=1, source_target_pairs={{4,8},{12,16},{20,24},{28,32},{36,40},{44,48},{52,56},{60,64},{68,... | collective-permute-start | bytes 196616 | tf_op jit(solution)/shard_map/ppermute | solution.py:400
  23.9 18.4 %all-to-all-start = ((f32[64,1,640]{2,1,0:T(1,128)}), f32[64,1,640]{2,1,0:T(1,128)S(1)}, u32[]{:S(2)}, u32[]{:S(2)}) async-start(f32[64,1,640]{2,1,0:T(1,128)} %get-tuple-element.31), calls=%async_computation | async-start | bytes 327680 | tf_op jit(solution)/shard_map/all_to_all | solution.py:437
  43.2 22.8 %all-to-all-start.1 = ((f32[64,1,640]{2,1,0:T(1,128)}), f32[64,1,640]{2,1,0:T(1,128)S(1)}, u32[]{:S(2)}, u32[]{:S(2)}) async-start(f32[64,1,640]{2,1,0:T(1,128)} %scan.1), calls=%async_computation.1 | async-start | bytes 327680 | tf_op jit(solution)/shard_map/all_to_all | solution.py:471
  52.3 13.7 %collective-permute-start.6 = (f32[32,1,1024]{2,1,0:T(1,128)S(1)}, f32[32,1,1024]{2,1,0:T(1,128)S(1)}, u32[]{:S(2)}, u32[]{:S(2)}) collective-permute-start(f32[32,1,1024]{2,1,0:T(1,128)S(1)} %get-tuple-element.40), channel_id=1, source_target_pairs={{0,1},{1,2},{2,3},{4,5},{5,6},{6,7},{8,9},{9,10},{10,11},{12,13},{... | collective-permute-start | bytes 393224 | tf_op jit(solution)/shard_map/ppermute | solution.py:401
  55.8 10.2 %collective-permute-start.7 = (f32[32,1,1024]{2,1,0:T(1,128)S(1)}, f32[32,1,1024]{2,1,0:T(1,128)S(1)}, u32[]{:S(2)}, u32[]{:S(2)}) collective-permute-start(f32[32,1,1024]{2,1,0:T(1,128)S(1)} %get-tuple-element.41), channel_id=1, source_target_pairs={{1,0},{2,1},{3,2},{5,4},{6,5},{7,6},{9,8},{10,9},{11,10},{13,12},{... | collective-permute-start | bytes 393224 | tf_op jit(solution)/shard_map/ppermute | solution.py:402
  58.2 5.1 %collective-permute-start.4 = (f32[16,1024]{1,0:T(8,128)S(1)}, f32[16,1024]{1,0:T(8,128)S(1)}, u32[]{:S(2)}, u32[]{:S(2)}) collective-permute-start(f32[16,1024]{1,0:T(8,128)S(1)} %get-tuple-element.38), channel_id=1, source_target_pairs={{0,4},{4,0},{1,5},{5,1},{2,6},{6,2},{3,7},{7,3},{8,12},{12,8},{9,1... | collective-permute-start | bytes 196616 | tf_op jit(solution)/shard_map/ppermute | solution.py:399
  58.3 7.7 %collective-permute-start.5 = (f32[16,1024]{1,0:T(8,128)S(1)}, f32[16,1024]{1,0:T(8,128)S(1)}, u32[]{:S(2)}, u32[]{:S(2)}) collective-permute-start(f32[16,1024]{1,0:T(8,128)S(1)} %get-tuple-element.39), channel_id=1, source_target_pairs={{4,8},{12,16},{20,24},{28,32},{36,40},{44,48},{52,56},{60,64},{68,... | collective-permute-start | bytes 196616 | tf_op jit(solution)/shard_map/ppermute | solution.py:400

commit v2 on v1

v2 whole, which is shorter than its diff:
```python
import functools

import jax
import jax.numpy as jnp
from jax import lax
from jax.experimental import pallas as pl
from jax.experimental.pallas import tpu as pltpu
from jax.sharding import Mesh
from jax.sharding import PartitionSpec as P

RAY = ("ray_0", "ray_1", "ray_2")
EXTINCTION = 0.7
LANES = 128
BLOCK = 8
PIECE = 4
VM = pl.BlockSpec(memory_space=pltpu.VMEM)
SM = pl.BlockSpec(memory_space=pltpu.SMEM)
HBM = pl.BlockSpec(memory_space=pltpu.HBM)


def sds(*shape):
    return jax.ShapeDtypeStruct(shape, jnp.float32)


def col(c):
    return pl.ds(c * LANES, LANES)


def half(h):
    return pl.ds(h * 8, 8)


def ids():
    lane = lax.broadcasted_iota(jnp.int32, (8, LANES), 1)
    sub = lax.broadcasted_iota(jnp.int32, (8, LANES), 0)
    return lane == 0, lane == LANES - 1, sub == 0, sub == 7


def wide(row):
    return jnp.broadcast_to(row, (8, LANES))


def col_neighbours(tiles, first, last):
    right = [pltpu.roll(t, 1, 1) for t in tiles]
    left = [pltpu.roll(t, LANES - 1, 1) for t in tiles]
    zero = jnp.zeros((8, LANES), jnp.float32)
    n = len(tiles)
    before = [jnp.where(first, right[c - 1] if c else zero, right[c]) for c in range(n)]
    after = [jnp.where(last, left[c + 1] if c < n - 1 else zero, left[c]) for c in range(n)]
    return before, after


def row_neighbours(top, bottom, above, below, first, last):
    down = [pltpu.roll(t, 1, 0) for t in (top, bottom)]
    up = [pltpu.roll(t, 7, 0) for t in (top, bottom)]
    before = (jnp.where(first, above, down[0]), jnp.where(first, down[0], down[1]))
    after = (jnp.where(last, up[1], up[0]), jnp.where(last, below, up[1]))
    return before, after


def absorbed(optical, terms):
    value = 1.0 - optical * (1.0 / terms)
    for n in range(terms - 1, 1, -1):
        value = 1.0 - optical * (1.0 / n) * value
    return optical * value


def gather_kernel(place, dens, cot, held, held_cot, row_one, row_two, to_near, to_cross, sems, cot_sem):
    ndep, nrow, _ = dens.shape
    core_first, row_first = place[0] == 0, place[1] == 0
    colours = pltpu.make_async_copy(cot, held_cot, cot_sem)
    copies = []
    for b in range(ndep // PIECE):
        part = pl.ds(b * PIECE, PIECE)
        copies.append(pltpu.make_async_copy(dens.at[part], held.at[part], sems.at[b]))
        copies[-1].start()
    colours.start()
    for b, copy in enumerate(copies):
        copy.wait()
        for k in range(b * PIECE, (b + 1) * PIECE):
            top, bottom = held[k, 0:1, :], held[k, nrow - 1 : nrow, :]
            row_one[k] = jnp.where(row_first, bottom, top)
            row_two[k] = jnp.where(row_first, top, bottom)
    first_layer, last_layer = held[0], held[ndep - 1]
    to_near[...] = jnp.where(core_first, last_layer, first_layer)
    to_cross[...] = jnp.where(core_first, first_layer, last_layer)
    colours.wait()


def facing(place, near, cross, one, two):
    core_first, row_first = place[0] == 0, place[1] == 0

    def layer(at, lower):
        a, b = near[at], cross[at]
        return jnp.where(core_first, b, a) if lower else jnp.where(core_first, a, b)

    def row(k, c, lower):
        a, b = one[k, :, col(c)], two[k, :, col(c)]
        return jnp.where(row_first, b, a) if lower else jnp.where(row_first, a, b)

    return layer, row


def shade(light, mid, before, after, lows, highs, masks):
    lx, ly, lz = light
    first, last, head, tail = masks
    nc = len(mid[0])
    zs = [col_neighbours(mid[h], first, last) for h in range(2)]
    out = [[None] * nc, [None] * nc]
    for c in range(nc):
        ys = row_neighbours(mid[0][c], mid[1][c], lows(c), highs(c), head, tail)
        for h in range(2):
            dx = after(h, c) - before(h, c)
            dy = ys[1][h] - ys[0][h]
            dz = zs[h][1][c] - zs[h][0][c]
            inv = lax.rsqrt(4.0 + dx * dx + dy * dy + dz * dz)
            out[h][c] = dx, dy, dz, inv, (lx * dx + ly * dy + lz * dz) * inv
    return out


def opacity(d, step):
    return d * (step - d * (step**2 / 2 - d * (step**3 / 6)))


def inner_kernel(step, light, dens, weight, square, lean, totals):
    ndep, _, ncol = dens.shape
    nc = ncol // LANES
    lx, lz = light[0], light[2]
    first, last, _, _ = ids()
    totals[0] = jnp.ones_like(totals[0])
    totals[1] = jnp.zeros_like(totals[1])

    def layer(k, inside=True):
        for h in range(2):
            mid = [dens[k, half(h), col(c)] for c in range(nc)]
            if inside:
                before, after = col_neighbours(mid, first, last)
            for c in range(nc):
                at = (half(h), col(c))
                t = totals[0, half(h), col(c)]
                w = t * opacity(mid[c], step)
                totals[0, half(h), col(c)] = t - w
                w = w * mid[c]
                weight[k, half(h), col(c)] = w
                totals[1, half(h), col(c)] += w
                if inside:
                    dx = dens[k + 1, half(h), col(c)] - dens[k - 1, half(h), col(c)]
                    dz = after[c] - before[c]
                    square[k, half(h), col(c)] = 4.0 + dx * dx + dz * dz
                    lean[k, half(h), col(c)] = lx * dx + lz * dz

    layer(0, False)
    pl.loop(1, ndep - 1, unroll=3)(layer)
    layer(ndep - 1, False)


def forward_kernel(
    step, place, light, tint, dens, cot, weight, square, lean, totals, near, cross, one, two,
    packed, ends, rho, colour, rims,
):
    ndep, _, ncol = dens.shape
    nc = ncol // LANES
    lights = light[0], light[1], light[2]
    masks = ids()
    outer, beyond = facing(place, near, cross, one, two)
    rims[...] = jnp.zeros_like(rims)
    colour[...] = totals[1]

    def edges(k):
        lows, highs = [beyond(k, c, True) for c in range(nc)], [beyond(k, c, False) for c in range(nc)]
        for c in range(nc):
            rims[0, :, col(c)] += lows[c]
            rims[1, :, col(c)] += highs[c]
        return lows, highs

    def outermost(k, before, after):
        lows, highs = edges(k)
        mid = [[dens[k, half(h), col(c)] for c in range(nc)] for h in range(2)]
        tiles = shade(
            lights, mid, before, after, lambda c: wide(lows[c]), lambda c: wide(highs[c]), masks
        )
        for c in range(nc):
            for h in range(2):
                colour[half(h), col(c)] += weight[k, half(h), col(c)] * tiles[h][c][4]

    def layer(k):
        lows, highs = edges(k)
        for c in range(nc):
            top, bottom = dens[k, half(0), col(c)], dens[k, half(1), col(c)]
            before, after = row_neighbours(
                top, bottom, wide(lows[c]), wide(highs[c]), masks[2], masks[3]
            )
            for h in range(2):
                cell = (k, half(h), col(c))
                dy = after[h] - before[h]
                inv = lax.rsqrt(square[cell] + dy * dy)
                colour[half(h), col(c)] += weight[cell] * ((lean[cell] + lights[1] * dy) * inv)

    outermost(
        0, lambda h, c: outer((half(h), col(c)), True), lambda h, c: dens[1, half(h), col(c)]
    )
    outermost(
        ndep - 1,
        lambda h, c: dens[ndep - 2, half(h), col(c)],
        lambda h, c: outer((half(h), col(c)), False),
    )
    pl.loop(1, ndep - 1, unroll=5)(layer)

    passed = [1.0 - absorbed(rims[n] * step, 7) for n in range(2)]
    for c in range(nc):
        cs = slice(c * LANES, (c + 1) * LANES)
        for h in range(2):
            at = (half(h), col(c))
            t, e = totals[0, half(h), col(c)], 0.5 * colour[at]
            r = cot[0, half(h), col(c)] * tint[0]
            r = r + cot[1, half(h), col(c)] * tint[1]
            r = r + cot[2, half(h), col(c)] * tint[2]
            rho[at] = r
            ends[0, half(h), col(c)] = t
            ends[1, half(h), col(c)] = e
            v = e * r
            for b in range(4):
                a = h * 4 + b
                p = a * nc + c
                packed[p, :, 0:128] = t[2 * b : 2 * b + 1]
                packed[p, :, 128:256] = t[2 * b + 1 : 2 * b + 2]
                packed[p, :, 256:384] = passed[a // 4][:, cs]
                packed[p, :, 384:512] = v[2 * b : 2 * b + 1]
                packed[p, :, 512:640] = v[2 * b + 1 : 2 * b + 2]


def adjoint_kernel(
    step, depth, place, light, dens, near, cross, one, two, rho, ends,
    parts, adj_y, adj_z, to_near, to_cross, row_one, row_two,
    held, xs, ys, zs, trans, colour, in_sems, y_sems, z_sems,
):
    ndep, _, ncol = dens.shape
    nc = ncol // LANES
    lx, ly, lz = lights = light[0], light[1], light[2]
    masks = ids()
    core_first, row_first = place[0] == 0, place[1] == 0
    outer, beyond = facing(place, near, cross, one, two)
    blocks = ndep // BLOCK
    arrivals = []
    for b in range(blocks):
        at = pl.ds(b * BLOCK, BLOCK)
        arrivals.append(
            pltpu.make_async_copy(dens.at[at], held.at[pl.ds(b * BLOCK + 1, BLOCK)], in_sems.at[b])
        )
        arrivals[-1].start()
    for c in range(nc):
        for h in range(2):
            at = (half(h), col(c))
            held[0, half(h), col(c)] = outer(at, True)
            held[ndep + 1, half(h), col(c)] = outer(at, False)
            trans[at] = jnp.ones((8, LANES), jnp.float32)
            colour[at] = jnp.zeros((8, LANES), jnp.float32)
            for k in (0, 1):
                xs[k, half(h), col(c)] = jnp.zeros((8, LANES), jnp.float32)
            parts[0, half(h), col(c)] = jnp.zeros((8, LANES), jnp.float32)

    def layer(k):
        mid = [[held[k + 1, half(h), col(c)] for c in range(nc)] for h in range(2)]
        tiles = shade(
            lights, mid,
            lambda h, c: held[k, half(h), col(c)], lambda h, c: held[k + 2, half(h), col(c)],
            lambda c: wide(beyond(k, c, True)), lambda c: wide(beyond(k, c, False)), masks,
        )
        for c in range(nc):
            outermost = []
            for h in range(2):
                at = (half(h), col(c))
                d = mid[h][c]
                dx, dy, dz, inv, q = tiles[h][c]
                lit = 0.5 + 0.5 * q
                t = trans[at]
                w = t * opacity(d, step)
                t = t - w
                trans[at] = t
                wd = w * d
                e = colour[at] + wd * lit
                colour[at] = e
                r = rho[at] * depth
                glow = r * (w * lit + step * (t * (d * lit) + e))
                s = wd * inv * (0.5 * r)
                m = q * inv
                x = s * (lx - m * dx)
                y = s * (ly - m * dy)
                xs[k + 2, half(h), col(c)] = x
                ys[k, half(h), col(c)] = y
                zs[k, half(h), col(c)] = s * (lz - m * dz)
                parts[k + 1, half(h), col(c)] = glow
                parts[k, half(h), col(c)] += xs[k, half(h), col(c)] - x
                outermost.append(y[7 * h : 7 * h + 1])
            top, bottom = outermost
            row_one[k, :, col(c)] = jnp.where(row_first, bottom, top)
            row_two[k, :, col(c)] = jnp.where(row_first, top, bottom)

    copies = []

    def send(source, target, start, count, sem):
        at = pl.ds(start, count)
        copies.append(pltpu.make_async_copy(source.at[at], target.at[at], sem))
        copies[-1].start()

    arrivals[0].wait()
    for b in range(blocks):
        if b < blocks - 1:
            arrivals[b + 1].wait()
        pl.loop(b * BLOCK, (b + 1) * BLOCK, unroll=4)(layer)
        send(ys, adj_y, b * BLOCK, BLOCK, y_sems.at[b])
        send(zs, adj_z, b * BLOCK, BLOCK, z_sems.at[b])
    for c in range(nc):
        for h in range(2):
            at = (half(h), col(c))
            parts[ndep, half(h), col(c)] += xs[ndep, half(h), col(c)]
            first_x = xs[2, half(h), col(c)]
            last_x = xs[ndep + 1, half(h), col(c)] / ends[0, half(h), col(c)]
            to_near[at] = jnp.where(core_first, last_x, first_x)
            to_cross[at] = jnp.where(core_first, first_x, last_x)
    for copy in copies:
        copy.wait()


def scan_kernel(packed, out):
    slabs = packed.shape[0]
    front = jnp.ones((1, 384), jnp.float32)
    for m in range(slabs):
        out[m, :, 0:384] = front
        if m < slabs - 1:
            front = front * packed[m, :, 0:384]
    behind = jnp.zeros((1, 256), jnp.float32)
    for m in reversed(range(slabs)):
        out[m, :, 384:640] = behind
        if m:
            behind = behind + out[m, :, 0:256] * packed[m, :, 384:640]


def combine_kernel(
    step, depth, place, scanned, x_near, x_cross, y_one, y_two, rho, ends, parts, adj_y, adj_z,
    out, front, base, edge, ys, zs, buf, y_sems, z_sems, out_sems,
):
    ndep, _, ncol = out.shape
    nc = ncol // LANES
    first, last, head, tail = ids()
    outer, beyond = facing(place, x_near, x_cross, y_one, y_two)
    blocks = ndep // BLOCK
    arrivals = []
    for b in range(blocks):
        at = pl.ds(b * BLOCK, BLOCK)
        arrivals.append(
            [
                pltpu.make_async_copy(source.at[at], target.at[at], sems.at[b])
                for source, target, sems in ((adj_y, ys, y_sems), (adj_z, zs, z_sems))
            ]
        )
        for copy in arrivals[-1]:
            copy.start()
    for c in range(nc):
        for a in range(8):
            p = a * nc + c
            front[2 * a : 2 * a + 1, col(c)] = scanned[p, :, 0:128]
            front[2 * a + 1 : 2 * a + 2, col(c)] = scanned[p, :, 128:256]
            base[2 * a : 2 * a + 1, col(c)] = scanned[p, :, 384:512]
            base[2 * a + 1 : 2 * a + 2, col(c)] = scanned[p, :, 512:640]
        edge[0, :, col(c)] = scanned[c, :, 256:384]
        edge[1, :, col(c)] = scanned[7 * nc + c, :, 256:384]
    for c in range(nc):
        for h in range(2):
            at = (half(h), col(c))
            base[at] = (depth * step) * (base[at] + front[at] * (rho[at] * ends[1, half(h), col(c)]))

    def layer(k):
        zt, yt = [[], []], [[], []]
        for h in range(2):
            for c in range(nc):
                f = front[half(h), col(c)]
                zt[h].append(f * zs[k, half(h), col(c)])
                yt[h].append(f * ys[k, half(h), col(c)])
        zn = [col_neighbours(zt[h], first, last) for h in range(2)]
        for c in range(nc):
            lo = wide(edge[0, :, col(c)] * beyond(k, c, True))
            hi = wide(edge[1, :, col(c)] * beyond(k, c, False))
            yn = row_neighbours(yt[0][c], yt[1][c], lo, hi, head, tail)
            for h in range(2):
                at, cell = (half(h), col(c)), (k, half(h), col(c))
                own = parts[k + 1, half(h), col(c)]
                buf[cell] = (front[at] * own - base[at]) + (
                    (yn[0][h] - yn[1][h]) + (zn[h][0][c] - zn[h][1][c])
                )

    copies = []
    for b in range(blocks):
        start, stop = b * BLOCK, (b + 1) * BLOCK
        for copy in arrivals[b]:
            copy.wait()
        pl.loop(start, stop, unroll=8)(layer)
        for c in range(nc):
            for h in range(2):
                at = (half(h), col(c))
                if b == 0:
                    buf[0, half(h), col(c)] += front[at] * outer(at, True)
                if stop == ndep:
                    x = outer(at, False) * ends[0, half(h), col(c)]
                    buf[ndep - 1, half(h), col(c)] -= front[at] * x
        at = pl.ds(b * BLOCK, BLOCK)
        copies.append(pltpu.make_async_copy(buf.at[at], out.at[at], out_sems.at[b]))
        copies[-1].start()
    for copy in copies:
        copy.wait()


def params(mib):
    return pltpu.CompilerParams(vmem_limit_bytes=mib << 20)


def cost(flops, nbytes):
    return pl.CostEstimate(flops=flops, bytes_accessed=nbytes, transcendentals=0)


def near_memory(*arrays):
    return [pltpu.with_memory_space_constraint(a, pltpu.VMEM) for a in arrays]


def far_memory(*arrays):
    return [pltpu.with_memory_space_constraint(a, pltpu.HBM) for a in arrays]


def local(density, light_dir, colour_tint, cotangent):
    ndep, nrow, ncol = density.shape
    slabs = lax.axis_size(RAY)
    rows = lax.axis_size("row")
    full_depth = float(ndep * slabs)
    step = EXTINCTION / full_depth
    place = jnp.stack([lax.axis_index(RAY[2]), lax.axis_index("row") % 2]).astype(jnp.int32)

    def pairs(start, stop):
        return [(i + n, i + 1 - n) for i in range(start, stop - 1, 2) for n in range(2)]

    def exchange(row_one, row_two, to_near, to_cross):
        return near_memory(
            lax.ppermute(to_near, RAY[2], pairs(0, 2)),
            lax.ppermute(to_cross, RAY, pairs(1, slabs)),
            lax.ppermute(row_one, "row", pairs(0, rows)),
            lax.ppermute(row_two, "row", pairs(1, rows)),
        )

    def vmem(*shape):
        return pltpu.VMEM(shape, jnp.float32)

    def hbm(*shape):
        return pltpu.HBM(shape, jnp.float32)

    cube, layer, rim = (ndep, nrow, ncol), (nrow, ncol), (ndep, 1, ncol)
    share = (slabs, 1, 5 * LANES)
    blocks = ndep // BLOCK
    cells = ndep * nrow * ncol
    sem = pltpu.SemaphoreType.DMA
    held, held_cot, *pieces = pl.pallas_call(
        gather_kernel,
        out_shape=(vmem(*cube), vmem(*cotangent.shape), vmem(*rim), vmem(*rim), vmem(*layer), vmem(*layer)),
        in_specs=[SM, HBM, HBM],
        out_specs=[VM] * 6,
        scratch_shapes=[sem((ndep // PIECE,)), sem],
        compiler_params=params(4),
        name="gather",
    )(place, *far_memory(density, cotangent))
    halos = exchange(*pieces)
    inner = pl.pallas_call(
        functools.partial(inner_kernel, step),
        out_shape=(vmem(*cube),) * 3 + (vmem(2, *layer),),
        in_specs=[SM, VM],
        out_specs=[VM] * 4,
        compiler_params=params(4),
        cost_estimate=cost(50 * cells, 16 * cells),
        name="inner",
    )(light_dir, held)
    packed, ends, rho = pl.pallas_call(
        functools.partial(forward_kernel, step),
        out_shape=(vmem(*share), vmem(2, *layer), vmem(*layer)),
        in_specs=[SM, SM, SM] + [VM] * 10,
        out_specs=[VM] * 3,
        scratch_shapes=[vmem(*layer), vmem(2, 1, ncol)],
        compiler_params=params(4),
        cost_estimate=cost(30 * cells, 4 * cells),
        name="forward",
    )(place, light_dir, colour_tint, held, held_cot, *inner, *halos)

    scanned = lax.all_to_all(packed, RAY, 0, 0)
    part, adj_y, adj_z, to_near, to_cross, row_one, row_two = pl.pallas_call(
        functools.partial(adjoint_kernel, step, full_depth),
        out_shape=(vmem(ndep + 1, nrow, ncol), hbm(*cube), hbm(*cube))
        + (vmem(*layer), vmem(*layer), vmem(*rim), vmem(*rim)),
        in_specs=[SM, SM, HBM] + [VM] * 6,
        out_specs=[VM, HBM, HBM] + [VM] * 4,
        scratch_shapes=[
            vmem(ndep + 2, nrow, ncol),
            vmem(ndep + 2, nrow, ncol),
            vmem(*cube),
            vmem(*cube),
            vmem(*layer),
            vmem(*layer),
            sem((blocks,)),
            sem((blocks,)),
            sem((blocks,)),
        ],
        compiler_params=params(16),
        cost_estimate=cost(70 * cells, 16 * cells),
        name="adjoint",
    )(place, light_dir, *far_memory(density), *halos, rho, ends)
    scanned, to_near, to_cross, row_one, row_two = lax.optimization_barrier(
        (scanned, to_near, to_cross, row_one, row_two)
    )
    scanned = pl.pallas_call(
        scan_kernel,
        out_shape=vmem(*share),
        in_specs=[VM],
        out_specs=VM,
        compiler_params=params(4),
        name="scan",
    )(*near_memory(scanned))
    scanned = lax.all_to_all(scanned, RAY, 0, 0)
    rims = exchange(row_one, row_two, to_near, to_cross)
    return pl.pallas_call(
        functools.partial(combine_kernel, step, full_depth),
        out_shape=sds(*cube),
        in_specs=[SM] + [VM] * 8 + [HBM] * 2,
        out_specs=HBM,
        scratch_shapes=[
            vmem(*layer),
            vmem(*layer),
            vmem(2, 1, ncol),
            vmem(*cube),
            vmem(*cube),
            vmem(*cube),
            sem((blocks,)),
            sem((blocks,)),
            sem((blocks,)),
        ],
        compiler_params=params(16),
        cost_estimate=cost(12 * cells, 16 * cells),
        name="combine",
    )(place, *near_memory(scanned), *rims, rho, ends, part, *far_memory(adj_y, adj_z))


def solution(mesh):
    torus = Mesh(
        mesh.devices.reshape(4, 8, 2, mesh.shape["row"]), ("ray_0", "ray_1", "ray_2", "row")
    )
    placed = (P(RAY, "row", None), P(), P(), P(None, "row", None))
    return jax.shard_map(
        local, mesh=torus, in_specs=placed, out_specs=P(RAY, "row", None), check_vma=False
    )
```

time: 72.3 us -> 62.7 us (0.87)
  starting transfers between devices: 43 us -> 37 us
  Pallas kernels: 22.2 us -> 19.7 us
  waiting for transfers between devices: 5.87 us -> 4.86 us
    ppermute x8, starting transfers between devices: 24.9 us -> 20.1 us  [the longest x2 12.9 us: exchange(): lax.ppermute(to_cross, RAY, pairs(1, slabs))]
    pallas_call x1, Pallas kernels: 5.04 us -> 2.63 us  [local(): pl.pallas_call(functools.partial(forward_kernel, step), out_shape=(vmem(*...]
    pallas_call x1 -> x2, Pallas kernels: 2.16 us -> 4.51 us  [the longest x1 2.34 us: local(): pl.pallas_call(functools.partial(inner_kernel, step), out_shape=(vmem(*cu...]
    pallas_call x1, Pallas kernels: 5.91 us -> 4.16 us  [local(): pl.pallas_call(functools.partial(combine_kernel, step, full_depth), out_s...]
    ppermute x8, waiting for transfers between devices: 4.67 us -> 2.92 us  [the longest x2 2.91 us: exchange(): lax.ppermute(to_cross, RAY, pairs(1, slabs))]
    pallas_call x1, Pallas kernels: 8.32 us -> 7.59 us  [local(): pl.pallas_call(functools.partial(adjoint_kernel, step, full_depth), out_s...]
    all_to_all x1, starting transfers between devices: 9.13 us -> 8.4 us  [local(): scanned = lax.all_to_all(scanned, RAY, 0, 0)]
    all_to_all x1, waiting for transfers between devices: 1.2 us -> 1.93 us  [local(): scanned = lax.all_to_all(packed, RAY, 0, 0)]
  transfers between devices with their start and end apart: 10 -> 10, of which waited for: 3 -> 2; matrix products, arithmetic and copies ran while one was open for 0% -> 0% of each run, Pallas kernels for 12% -> 16%
where the time goes in v2:
time: 62.7 us; the launch traced here: 61.7 us
  starting transfers between devices  37 us (59%)
  Pallas kernels  19.7 us (31%)
  waiting for transfers between devices  4.86 us (8%)
    ppermute x2, starting transfers between devices, exchange(): lax.ppermute(to_cross, RAY, pairs(1, slabs))  12.9 us
    all_to_all x1, starting transfers between devices, local(): scanned = lax.all_to_all(packed, RAY, 0, 0)  8.44 us
    all_to_all x1, starting transfers between devices, local(): scanned = lax.all_to_all(scanned, RAY, 0, 0)  8.4 us
    pallas_call x1, Pallas kernels, local(): pl.pallas_call(functools.partial(adjoint_kernel, step, full_depth), out_s...  7.59 us
    ppermute x2, starting transfers between devices, exchange(): lax.ppermute(row_two, 'row', pairs(1, rows))  6.23 us
    pallas_call x1, Pallas kernels, local(): pl.pallas_call(functools.partial(combine_kernel, step, full_depth), out_s...  4.16 us
    ppermute x2, waiting for transfers between devices, exchange(): lax.ppermute(to_cross, RAY, pairs(1, slabs))  2.91 us
    pallas_call x1, Pallas kernels, local(): pl.pallas_call(functools.partial(forward_kernel, step), out_shape=(vmem(*...  2.63 us
  transfers between devices with their start and end apart: 10, of which 2 were waited for; matrix products, arithmetic and copies ran while one was open for 0% of the time, Pallas kernels for 16%

profile of v2, /device:TPU:14, one launch (start us, length us, event | category | flops | bytes accessed | tf_op | source)
XLA Modules:
  0.0 61.7 jit_solution(6895353181076022211)
XLA Ops:
  0.0 0.1 pad_add_fusion.place
  0.1 2.2 %gather.1 = (f32[32,16,1024]{2,1,0:T(8,128)S(1)}, f32[3,16,1024]{2,1,0:T(8,128)S(1)}, f32[32,1,1024]{2,1,0:T(1,128)S(1)}, f32[32,1,1024]{2,1,0:T(1,128)S(1)}, f3...) custom-call(s32[2]{0:T(128)S(1)} %pad_add_fusion.place, f32[32,16,1024]{2,1,0:T(8,128)} %dens.3, f32[3,16,1024]{2,1,0:T(8,128)} %cot.1), custom_call_target="tpu_custom_call" | custom-call | tf_op jit(solution)/shard_map/gather/pallas_call | solution.py:459
  2.3 0.5 collective-permute-start.2
  2.8 4.3 %collective-permute-start.3 = (f32[32,1,1024]{2,1,0:T(1,128)S(1)}, f32[32,1,1024]{2,1,0:T(1,128)S(1)}, u32[]{:S(2)}, u32[]{:S(2)}) collective-permute-start(f32[32,1,1024]{2,1,0:T(1,128)S(1)} %get-tuple-element.39), channel_id=1, source_target_pairs={{1,2},{2,1},{5,6},{6,5},{9,10},{10,9},{13,14},{14,13},{17,18},{18,... | collective-permute-start | bytes 393224 | tf_op jit(solution)/shard_map/ppermute | solution.py:445
  7.1 0.1 collective-permute-start
  7.2 8.1 %collective-permute-start.1 = (f32[16,1024]{1,0:T(8,128)S(1)}, f32[16,1024]{1,0:T(8,128)S(1)}, u32[]{:S(2)}, u32[]{:S(2)}) collective-permute-start(f32[16,1024]{1,0:T(8,128)S(1)} %get-tuple-element.37), channel_id=1, source_target_pairs={{4,8},{8,4},{12,16},{16,12},{20,24},{24,20},{28,32},{32,28},{36,40... | collective-permute-start | bytes 196616 | tf_op jit(solution)/shard_map/ppermute | solution.py:443
  15.4 2.3 %inner.1 = (f32[32,16,1024]{2,1,0:T(8,128)S(1)}, f32[32,16,1024]{2,1,0:T(8,128)S(1)}, f32[32,16,1024]{2,1,0:T(8,128)S(1)}, f32[2,16,1024]{2,1,0:T(8,128)S(1)}) custom-call(f32[3]{0:T(128)S(1)} %copy-done, f32[32,16,1024]{2,1,0:T(8,128)S(1)} %get-tuple-element.30.dens), custom_call_target="tpu_custom_call" | custom-call | flops 26214400 | bytes 8388608 | tf_op jit(solution)/shard_map/inner/pallas_call | solution.py:469
  17.7 0.0 collective-permute-done.near
  17.7 0.0 collective-permute-done.1.cross
  17.7 0.0 collective-permute-done.2.one
  17.7 0.0 collective-permute-done.3.two
  17.7 2.6 %forward.1 = (f32[64,1,640]{2,1,0:T(1,128)}, f32[2,16,1024]{2,1,0:T(8,128)S(1)}, f32[16,1024]{1,0:T(8,128)S(1)}) custom-call(s32[2]{0:T(128)S(1)} %pad_add_fusion.place, f32[3]{0:T(128)S(1)} %copy-done, f32[3]{0:T(128)S(1)} %copy-done.1, f32[32,16,1024]{2,1,0:T(8,128)S(1)} %get-tuple-element.30.dens, f32[3,16,1024]{2,1,0:T(8,128)S(1)} %get-tuple-element.31.cot, ...), custom_call_target="tpu_custom_call" | custom-call | flops 15728640 | bytes 2097152 | tf_op jit(solution)/shard_map/forward/pallas_call | solution.py:478
  20.4 8.4 %all-to-all-start = ((f32[64,1,640]{2,1,0:T(1,128)}), f32[64,1,640]{2,1,0:T(1,128)S(1)}, u32[]{:S(2)}, u32[]{:S(2)}) async-start(f32[64,1,640]{2,1,0:T(1,128)} %get-tuple-element.40), calls=%async_computation | async-start | bytes 327680 | tf_op jit(solution)/shard_map/all_to_all | solution.py:489
  28.8 7.6 %adjoint.1 = (f32[33,16,1024]{2,1,0:T(8,128)S(1)}, f32[32,16,1024]{2,1,0:T(8,128)}, f32[32,16,1024]{2,1,0:T(8,128)}, f32[16,1024]{1,0:T(8,128)S(1)}, f32[16,1024...) custom-call(s32[2]{0:T(128)S(1)} %pad_add_fusion.place, f32[3]{0:T(128)S(1)} %copy-done, ...), custom_call_target="tpu_custom_call" | custom-call | flops 36700160 | bytes 8388608 | tf_op jit(solution)/shard_map/adjoint/pallas_call | solution.py:490
  36.4 1.9 %all-to-all-done.packed = f32[64,1,640]{2,1,0:T(1,128)S(1)} async-done(((f32[64,1,640]{2,1,0:T(1,128)}), f32[64,1,640]{2,1,0:T(1,128)S(1)}, u32[]{:S(2)}, u32[]{:S(2)}) %all-to-all-start) | async-done | bytes 163872 | tf_op jit(solution)/shard_map/all_to_all | solution.py:489
  38.4 0.8 %scan.1 = f32[64,1,640]{2,1,0:T(1,128)} custom-call(f32[64,1,640]{2,1,0:T(1,128)S(1)} %all-to-all-done.packed), custom_call_target="tpu_custom_call" | custom-call | tf_op jit(solution)/shard_map/scan/pallas_call | solution.py:514
  39.2 8.4 %all-to-all-start.1 = ((f32[64,1,640]{2,1,0:T(1,128)}), f32[64,1,640]{2,1,0:T(1,128)S(1)}, u32[]{:S(2)}, u32[]{:S(2)}) async-start(f32[64,1,640]{2,1,0:T(1,128)} %scan.1), calls=%async_computation.1 | async-start | bytes 327680 | tf_op jit(solution)/shard_map/all_to_all | solution.py:522
  47.6 0.1 collective-permute-start.6
  47.7 1.9 %collective-permute-start.7 = (f32[32,1,1024]{2,1,0:T(1,128)S(1)}, f32[32,1,1024]{2,1,0:T(1,128)S(1)}, u32[]{:S(2)}, u32[]{:S(2)}) collective-permute-start(f32[32,1,1024]{2,1,0:T(1,128)S(1)} %get-tuple-element.51), channel_id=1, source_target_pairs={{1,2},{2,1},{5,6},{6,5},{9,10},{10,9},{13,14},{14,13},{17,18},{18,... | collective-permute-start | bytes 393224 | tf_op jit(solution)/shard_map/ppermute | solution.py:445
  49.6 0.2 collective-permute-start.4
  49.8 4.8 %collective-permute-start.5 = (f32[16,1024]{1,0:T(8,128)S(1)}, f32[16,1024]{1,0:T(8,128)S(1)}, u32[]{:S(2)}, u32[]{:S(2)}) collective-permute-start(f32[16,1024]{1,0:T(8,128)S(1)} %get-tuple-element.49), channel_id=1, source_target_pairs={{4,8},{8,4},{12,16},{16,12},{20,24},{24,20},{28,32},{32,28},{36,40... | collective-permute-start | bytes 196616 | tf_op jit(solution)/shard_map/ppermute | solution.py:443
  54.7 2.9 %collective-permute-done.5.x_cross = f32[16,1024]{1,0:T(8,128)S(1)} collective-permute-done((f32[16,1024]{1,0:T(8,128)S(1)}, f32[16,1024]{1,0:T(8,128)S(1)}, u32[]{:S(2)}, u32[]{:S(2)}) %collective-permute-start.5) | collective-permute-done | bytes 65568 | tf_op jit(solution)/shard_map/ppermute | solution.py:443
  57.6 0.0 all-to-all-done.1.scanned
  57.6 4.2 %combine.1 = f32[32,16,1024]{2,1,0:T(8,128)} custom-call(s32[2]{0:T(128)S(1)} %pad_add_fusion.place, f32[64,1,640]{2,1,0:T(1,128)S(1)} %all-to-all-done.1.scanned, f32[16,1024]{1,0:T(8,128)S(1)} %collective-permute-done.4.x_near, f32[16,1024]{1,0:T(8,128)S(1)} %collective-permute-done.5.x_cross, f32[32,1,1024]{2,1,0:T(1,128)S(1)} %collective-permute-done.6.y_one, ...), custom_call_target="tpu_custom_call" | custom-call | flops 6291456 | bytes 8388608 | tf_op jit(solution)/shard_map/combine/pallas_call | solution.py:524
  (7 shorter events, 0.0 us)
Async XLA Ops:
  0.0 15.3 %copy-start = (f32[3]{0:T(128)S(1)}, f32[3]{0:T(128)}, u32[]{:S(2)}) copy-start(f32[3]{0:T(128)} %light.5) | copy-start | bytes 40
  0.1 17.7 %copy-start.1 = (f32[3]{0:T(128)S(1)}, f32[3]{0:T(128)}, u32[]{:S(2)}) copy-start(f32[3]{0:T(128)} %tint.1) | copy-start | bytes 40
  2.3 15.5 %collective-permute-start.2 = (f32[32,1,1024]{2,1,0:T(1,128)S(1)}, f32[32,1,1024]{2,1,0:T(1,128)S(1)}, u32[]{:S(2)}, u32[]{:S(2)}) collective-permute-start(f32[32,1,1024]{2,1,0:T(1,128)S(1)} %get-tuple-element.38), channel_id=1, source_target_pairs={{0,1},{1,0},{2,3},{3,2},{4,5},{5,4},{6,7},{7,6},{8,9},{9,8},{10,11... | collective-permute-start | bytes 393224 | tf_op jit(solution)/shard_map/ppermute | solution.py:444
  2.8 14.9 %collective-permute-start.3 = (f32[32,1,1024]{2,1,0:T(1,128)S(1)}, f32[32,1,1024]{2,1,0:T(1,128)S(1)}, u32[]{:S(2)}, u32[]{:S(2)}) collective-permute-start(f32[32,1,1024]{2,1,0:T(1,128)S(1)} %get-tuple-element.39), channel_id=1, source_target_pairs={{1,2},{2,1},{5,6},{6,5},{9,10},{10,9},{13,14},{14,13},{17,18},{18,... | collective-permute-start | bytes 393224 | tf_op jit(solution)/shard_map/ppermute | solution.py:445
  7.1 10.6 %collective-permute-start = (f32[16,1024]{1,0:T(8,128)S(1)}, f32[16,1024]{1,0:T(8,128)S(1)}, u32[]{:S(2)}, u32[]{:S(2)}) collective-permute-start(f32[16,1024]{1,0:T(8,128)S(1)} %get-tuple-element.36), channel_id=1, source_target_pairs={{0,4},{4,0},{1,5},{5,1},{2,6},{6,2},{3,7},{7,3},{8,12},{12,8},{9,1... | collective-permute-start | bytes 196616 | tf_op jit(solution)/shard_map/ppermute | solution.py:442
  7.2 10.5 %collective-permute-start.1 = (f32[16,1024]{1,0:T(8,128)S(1)}, f32[16,1024]{1,0:T(8,128)S(1)}, u32[]{:S(2)}, u32[]{:S(2)}) collective-permute-start(f32[16,1024]{1,0:T(8,128)S(1)} %get-tuple-element.37), channel_id=1, source_target_pairs={{4,8},{8,4},{12,16},{16,12},{20,24},{24,20},{28,32},{32,28},{36,40... | collective-permute-start | bytes 196616 | tf_op jit(solution)/shard_map/ppermute | solution.py:443
  20.4 18.0 %all-to-all-start = ((f32[64,1,640]{2,1,0:T(1,128)}), f32[64,1,640]{2,1,0:T(1,128)S(1)}, u32[]{:S(2)}, u32[]{:S(2)}) async-start(f32[64,1,640]{2,1,0:T(1,128)} %get-tuple-element.40), calls=%async_computation | async-start | bytes 327680 | tf_op jit(solution)/shard_map/all_to_all | solution.py:489
  39.2 18.4 %all-to-all-start.1 = ((f32[64,1,640]{2,1,0:T(1,128)}), f32[64,1,640]{2,1,0:T(1,128)S(1)}, u32[]{:S(2)}, u32[]{:S(2)}) async-start(f32[64,1,640]{2,1,0:T(1,128)} %scan.1), calls=%async_computation.1 | async-start | bytes 327680 | tf_op jit(solution)/shard_map/all_to_all | solution.py:522
  47.6 10.0 %collective-permute-start.6 = (f32[32,1,1024]{2,1,0:T(1,128)S(1)}, f32[32,1,1024]{2,1,0:T(1,128)S(1)}, u32[]{:S(2)}, u32[]{:S(2)}) collective-permute-start(f32[32,1,1024]{2,1,0:T(1,128)S(1)} %get-tuple-element.50), channel_id=1, source_target_pairs={{0,1},{1,0},{2,3},{3,2},{4,5},{5,4},{6,7},{7,6},{8,9},{9,8},{10,11... | collective-permute-start | bytes 393224 | tf_op jit(solution)/shard_map/ppermute | solution.py:444
  47.7 9.9 %collective-permute-start.7 = (f32[32,1,1024]{2,1,0:T(1,128)S(1)}, f32[32,1,1024]{2,1,0:T(1,128)S(1)}, u32[]{:S(2)}, u32[]{:S(2)}) collective-permute-start(f32[32,1,1024]{2,1,0:T(1,128)S(1)} %get-tuple-element.51), channel_id=1, source_target_pairs={{1,2},{2,1},{5,6},{6,5},{9,10},{10,9},{13,14},{14,13},{17,18},{18,... | collective-permute-start | bytes 393224 | tf_op jit(solution)/shard_map/ppermute | solution.py:445
  49.6 5.1 %collective-permute-start.4 = (f32[16,1024]{1,0:T(8,128)S(1)}, f32[16,1024]{1,0:T(8,128)S(1)}, u32[]{:S(2)}, u32[]{:S(2)}) collective-permute-start(f32[16,1024]{1,0:T(8,128)S(1)} %get-tuple-element.48), channel_id=1, source_target_pairs={{0,4},{4,0},{1,5},{5,1},{2,6},{6,2},{3,7},{7,3},{8,12},{12,8},{9,1... | collective-permute-start | bytes 196616 | tf_op jit(solution)/shard_map/ppermute | solution.py:442
  49.8 7.7 %collective-permute-start.5 = (f32[16,1024]{1,0:T(8,128)S(1)}, f32[16,1024]{1,0:T(8,128)S(1)}, u32[]{:S(2)}, u32[]{:S(2)}) collective-permute-start(f32[16,1024]{1,0:T(8,128)S(1)} %get-tuple-element.49), channel_id=1, source_target_pairs={{4,8},{8,4},{12,16},{16,12},{20,24},{24,20},{28,32},{32,28},{36,40... | collective-permute-start | bytes 196616 | tf_op jit(solution)/shard_map/ppermute | solution.py:443

commit v3 on v2

--- a/solution.py
+++ b/solution.py
@@ -13,6 +13,7 @@
 LANES = 128
 BLOCK = 8
 PIECE = 4
+CUTS = (0, 4, 12, 20, 28, 32)
 VM = pl.BlockSpec(memory_space=pltpu.VMEM)
 SM = pl.BlockSpec(memory_space=pltpu.SMEM)
 HBM = pl.BlockSpec(memory_space=pltpu.HBM)
@@ -150,7 +151,7 @@
                     lean[k, half(h), col(c)] = lx * dx + lz * dz
 
     layer(0, False)
-    pl.loop(1, ndep - 1, unroll=3)(layer)
+    pl.loop(1, ndep - 1, unroll=6)(layer)
     layer(ndep - 1, False)
 
 
@@ -204,7 +205,7 @@
         lambda h, c: dens[ndep - 2, half(h), col(c)],
         lambda h, c: outer((half(h), col(c)), False),
     )
-    pl.loop(1, ndep - 1, unroll=5)(layer)
+    pl.loop(1, ndep - 1, unroll=10)(layer)
 
     passed = [1.0 - absorbed(rims[n] * step, 7) for n in range(2)]
     for c in range(nc):
@@ -325,15 +326,15 @@
 def scan_kernel(packed, out):
     slabs = packed.shape[0]
     front = jnp.ones((1, 384), jnp.float32)
+    weighed = []
     for m in range(slabs):
         out[m, :, 0:384] = front
-        if m < slabs - 1:
-            front = front * packed[m, :, 0:384]
+        weighed.append(front[:, :256] * packed[m, :, 384:640])
+        front = front * packed[m, :, 0:384]
     behind = jnp.zeros((1, 256), jnp.float32)
     for m in reversed(range(slabs)):
         out[m, :, 384:640] = behind
-        if m:
-            behind = behind + out[m, :, 0:256] * packed[m, :, 384:640]
+        behind = behind + weighed[m]
 
 
 def combine_kernel(
@@ -344,10 +345,10 @@
     nc = ncol // LANES
     first, last, head, tail = ids()
     outer, beyond = facing(place, x_near, x_cross, y_one, y_two)
-    blocks = ndep // BLOCK
+    spans = list(zip(CUTS[:-1], CUTS[1:]))
     arrivals = []
-    for b in range(blocks):
-        at = pl.ds(b * BLOCK, BLOCK)
+    for b, (start, stop) in enumerate(spans):
+        at = pl.ds(start, stop - start)
         arrivals.append(
             [
                 pltpu.make_async_copy(source.at[at], target.at[at], sems.at[b])
@@ -390,11 +391,10 @@
                 )
 
     copies = []
-    for b in range(blocks):
-        start, stop = b * BLOCK, (b + 1) * BLOCK
+    for b, (start, stop) in enumerate(spans):
         for copy in arrivals[b]:
             copy.wait()
-        pl.loop(start, stop, unroll=8)(layer)
+        pl.loop(start, stop, unroll=stop - start)(layer)
         for c in range(nc):
             for h in range(2):
                 at = (half(h), col(c))
@@ -403,7 +403,7 @@
                 if stop == ndep:
                     x = outer(at, False) * ends[0, half(h), col(c)]
                     buf[ndep - 1, half(h), col(c)] -= front[at] * x
-        at = pl.ds(b * BLOCK, BLOCK)
+        at = pl.ds(start, stop - start)
         copies.append(pltpu.make_async_copy(buf.at[at], out.at[at], out_sems.at[b]))
         copies[-1].start()
     for copy in copies:
@@ -533,9 +533,9 @@
             vmem(*cube),
             vmem(*cube),
             vmem(*cube),
-            sem((blocks,)),
-            sem((blocks,)),
-            sem((blocks,)),
+            sem((len(CUTS),)),
+            sem((len(CUTS),)),
+            sem((len(CUTS),)),
         ],
         compiler_params=params(16),
         cost_estimate=cost(12 * cells, 16 * cells),

time: 62.7 us -> 62.6 us (level)
  no operation moved by 1% of the time
where the time goes in v3:
time: 62.6 us; the launch traced here: 61.7 us
  starting transfers between devices  37.2 us (59%)
  Pallas kernels  19.3 us (31%)
  waiting for transfers between devices  4.86 us (8%)
    ppermute x2, starting transfers between devices, exchange(): lax.ppermute(to_cross, RAY, pairs(1, slabs))  12.9 us
    all_to_all x1, starting transfers between devices, local(): scanned = lax.all_to_all(packed, RAY, 0, 0)  8.73 us
    all_to_all x1, starting transfers between devices, local(): scanned = lax.all_to_all(scanned, RAY, 0, 0)  8.4 us
    pallas_call x1, Pallas kernels, local(): pl.pallas_call(functools.partial(adjoint_kernel, step, full_depth), out_s...  7.59 us
    ppermute x2, starting transfers between devices, exchange(): lax.ppermute(row_two, 'row', pairs(1, rows))  6.23 us
    pallas_call x1, Pallas kernels, local(): pl.pallas_call(functools.partial(combine_kernel, step, full_depth), out_s...  4.12 us
    ppermute x2, waiting for transfers between devices, exchange(): lax.ppermute(to_cross, RAY, pairs(1, slabs))  2.91 us
    pallas_call x1, Pallas kernels, local(): pl.pallas_call(functools.partial(forward_kernel, step), out_shape=(vmem(*...  2.6 us
  transfers between devices with their start and end apart: 10, of which 2 were waited for; matrix products, arithmetic and copies ran while one was open for 0% of the time, Pallas kernels for 16%

profile of v3, /device:TPU:14, one launch (start us, length us, event | category | flops | bytes accessed | tf_op | source)
XLA Modules:
  0.0 61.7 jit_solution(13877649992970105365)
XLA Ops:
  0.0 0.1 pad_add_fusion.place
  0.1 2.2 %gather.1 = (f32[32,16,1024]{2,1,0:T(8,128)S(1)}, f32[3,16,1024]{2,1,0:T(8,128)S(1)}, f32[32,1,1024]{2,1,0:T(1,128)S(1)}, f32[32,1,1024]{2,1,0:T(1,128)S(1)}, f3...) custom-call(s32[2]{0:T(128)S(1)} %pad_add_fusion.place, f32[32,16,1024]{2,1,0:T(8,128)} %dens.3, f32[3,16,1024]{2,1,0:T(8,128)} %cot.1), custom_call_target="tpu_custom_call" | custom-call | tf_op jit(solution)/shard_map/gather/pallas_call | solution.py:459
  2.3 0.5 collective-permute-start.2
  2.8 4.3 %collective-permute-start.3 = (f32[32,1,1024]{2,1,0:T(1,128)S(1)}, f32[32,1,1024]{2,1,0:T(1,128)S(1)}, u32[]{:S(2)}, u32[]{:S(2)}) collective-permute-start(f32[32,1,1024]{2,1,0:T(1,128)S(1)} %get-tuple-element.39), channel_id=1, source_target_pairs={{1,2},{2,1},{5,6},{6,5},{9,10},{10,9},{13,14},{14,13},{17,18},{18,... | collective-permute-start | bytes 393224 | tf_op jit(solution)/shard_map/ppermute | solution.py:445
  7.1 0.1 collective-permute-start
  7.2 8.1 %collective-permute-start.1 = (f32[16,1024]{1,0:T(8,128)S(1)}, f32[16,1024]{1,0:T(8,128)S(1)}, u32[]{:S(2)}, u32[]{:S(2)}) collective-permute-start(f32[16,1024]{1,0:T(8,128)S(1)} %get-tuple-element.37), channel_id=1, source_target_pairs={{4,8},{8,4},{12,16},{16,12},{20,24},{24,20},{28,32},{32,28},{36,40... | collective-permute-start | bytes 196616 | tf_op jit(solution)/shard_map/ppermute | solution.py:443
  15.4 2.0 %inner.1 = (f32[32,16,1024]{2,1,0:T(8,128)S(1)}, f32[32,16,1024]{2,1,0:T(8,128)S(1)}, f32[32,16,1024]{2,1,0:T(8,128)S(1)}, f32[2,16,1024]{2,1,0:T(8,128)S(1)}) custom-call(f32[3]{0:T(128)S(1)} %copy-done, f32[32,16,1024]{2,1,0:T(8,128)S(1)} %get-tuple-element.30.dens), custom_call_target="tpu_custom_call" | custom-call | flops 26214400 | bytes 8388608 | tf_op jit(solution)/shard_map/inner/pallas_call | solution.py:469
  17.4 0.0 collective-permute-done.near
  17.4 0.0 collective-permute-done.1.cross
  17.4 0.0 collective-permute-done.2.one
  17.4 0.0 collective-permute-done.3.two
  17.5 2.6 %forward.1 = (f32[64,1,640]{2,1,0:T(1,128)}, f32[2,16,1024]{2,1,0:T(8,128)S(1)}, f32[16,1024]{1,0:T(8,128)S(1)}) custom-call(s32[2]{0:T(128)S(1)} %pad_add_fusion.place, f32[3]{0:T(128)S(1)} %copy-done, f32[3]{0:T(128)S(1)} %copy-done.1, f32[32,16,1024]{2,1,0:T(8,128)S(1)} %get-tuple-element.30.dens, f32[3,16,1024]{2,1,0:T(8,128)S(1)} %get-tuple-element.31.cot, ...), custom_call_target="tpu_custom_call" | custom-call | flops 15728640 | bytes 2097152 | tf_op jit(solution)/shard_map/forward/pallas_call | solution.py:478
  20.1 8.7 %all-to-all-start = ((f32[64,1,640]{2,1,0:T(1,128)}), f32[64,1,640]{2,1,0:T(1,128)S(1)}, u32[]{:S(2)}, u32[]{:S(2)}) async-start(f32[64,1,640]{2,1,0:T(1,128)} %get-tuple-element.40), calls=%async_computation | async-start | bytes 327680 | tf_op jit(solution)/shard_map/all_to_all | solution.py:489
  28.8 7.6 %adjoint.1 = (f32[33,16,1024]{2,1,0:T(8,128)S(1)}, f32[32,16,1024]{2,1,0:T(8,128)}, f32[32,16,1024]{2,1,0:T(8,128)}, f32[16,1024]{1,0:T(8,128)S(1)}, f32[16,1024...) custom-call(s32[2]{0:T(128)S(1)} %pad_add_fusion.place, f32[3]{0:T(128)S(1)} %copy-done, ...), custom_call_target="tpu_custom_call" | custom-call | flops 36700160 | bytes 8388608 | tf_op jit(solution)/shard_map/adjoint/pallas_call | solution.py:490
  36.4 1.9 %all-to-all-done.packed = f32[64,1,640]{2,1,0:T(1,128)S(1)} async-done(((f32[64,1,640]{2,1,0:T(1,128)}), f32[64,1,640]{2,1,0:T(1,128)S(1)}, u32[]{:S(2)}, u32[]{:S(2)}) %all-to-all-start) | async-done | bytes 163872 | tf_op jit(solution)/shard_map/all_to_all | solution.py:489
  38.3 0.8 %scan.1 = f32[64,1,640]{2,1,0:T(1,128)} custom-call(f32[64,1,640]{2,1,0:T(1,128)S(1)} %all-to-all-done.packed), custom_call_target="tpu_custom_call" | custom-call | tf_op jit(solution)/shard_map/scan/pallas_call | solution.py:514
  39.1 8.4 %all-to-all-start.1 = ((f32[64,1,640]{2,1,0:T(1,128)}), f32[64,1,640]{2,1,0:T(1,128)S(1)}, u32[]{:S(2)}, u32[]{:S(2)}) async-start(f32[64,1,640]{2,1,0:T(1,128)} %scan.1), calls=%async_computation.1 | async-start | bytes 327680 | tf_op jit(solution)/shard_map/all_to_all | solution.py:522
  47.5 0.1 collective-permute-start.6
  47.6 1.9 %collective-permute-start.7 = (f32[32,1,1024]{2,1,0:T(1,128)S(1)}, f32[32,1,1024]{2,1,0:T(1,128)S(1)}, u32[]{:S(2)}, u32[]{:S(2)}) collective-permute-start(f32[32,1,1024]{2,1,0:T(1,128)S(1)} %get-tuple-element.51), channel_id=1, source_target_pairs={{1,2},{2,1},{5,6},{6,5},{9,10},{10,9},{13,14},{14,13},{17,18},{18,... | collective-permute-start | bytes 393224 | tf_op jit(solution)/shard_map/ppermute | solution.py:445
  49.6 0.2 collective-permute-start.4
  49.8 4.8 %collective-permute-start.5 = (f32[16,1024]{1,0:T(8,128)S(1)}, f32[16,1024]{1,0:T(8,128)S(1)}, u32[]{:S(2)}, u32[]{:S(2)}) collective-permute-start(f32[16,1024]{1,0:T(8,128)S(1)} %get-tuple-element.49), channel_id=1, source_target_pairs={{4,8},{8,4},{12,16},{16,12},{20,24},{24,20},{28,32},{32,28},{36,40... | collective-permute-start | bytes 196616 | tf_op jit(solution)/shard_map/ppermute | solution.py:443
  54.6 2.9 %collective-permute-done.5.x_cross = f32[16,1024]{1,0:T(8,128)S(1)} collective-permute-done((f32[16,1024]{1,0:T(8,128)S(1)}, f32[16,1024]{1,0:T(8,128)S(1)}, u32[]{:S(2)}, u32[]{:S(2)}) %collective-permute-start.5) | collective-permute-done | bytes 65568 | tf_op jit(solution)/shard_map/ppermute | solution.py:443
  57.5 0.0 all-to-all-done.1.scanned
  57.5 4.1 %combine.1 = f32[32,16,1024]{2,1,0:T(8,128)} custom-call(s32[2]{0:T(128)S(1)} %pad_add_fusion.place, f32[64,1,640]{2,1,0:T(1,128)S(1)} %all-to-all-done.1.scanned, f32[16,1024]{1,0:T(8,128)S(1)} %collective-permute-done.4.x_near, f32[16,1024]{1,0:T(8,128)S(1)} %collective-permute-done.5.x_cross, f32[32,1,1024]{2,1,0:T(1,128)S(1)} %collective-permute-done.6.y_one, ...), custom_call_target="tpu_custom_call" | custom-call | flops 6291456 | bytes 8388608 | tf_op jit(solution)/shard_map/combine/pallas_call | solution.py:524
  (7 shorter events, 0.0 us)
Async XLA Ops:
  0.0 15.3 %copy-start = (f32[3]{0:T(128)S(1)}, f32[3]{0:T(128)}, u32[]{:S(2)}) copy-start(f32[3]{0:T(128)} %light.5) | copy-start | bytes 40
  0.1 17.4 %copy-start.1 = (f32[3]{0:T(128)S(1)}, f32[3]{0:T(128)}, u32[]{:S(2)}) copy-start(f32[3]{0:T(128)} %tint.1) | copy-start | bytes 40
  2.3 15.2 %collective-permute-start.2 = (f32[32,1,1024]{2,1,0:T(1,128)S(1)}, f32[32,1,1024]{2,1,0:T(1,128)S(1)}, u32[]{:S(2)}, u32[]{:S(2)}) collective-permute-start(f32[32,1,1024]{2,1,0:T(1,128)S(1)} %get-tuple-element.38), channel_id=1, source_target_pairs={{0,1},{1,0},{2,3},{3,2},{4,5},{5,4},{6,7},{7,6},{8,9},{9,8},{10,11... | collective-permute-start | bytes 393224 | tf_op jit(solution)/shard_map/ppermute | solution.py:444
  2.8 14.6 %collective-permute-start.3 = (f32[32,1,1024]{2,1,0:T(1,128)S(1)}, f32[32,1,1024]{2,1,0:T(1,128)S(1)}, u32[]{:S(2)}, u32[]{:S(2)}) collective-permute-start(f32[32,1,1024]{2,1,0:T(1,128)S(1)} %get-tuple-element.39), channel_id=1, source_target_pairs={{1,2},{2,1},{5,6},{6,5},{9,10},{10,9},{13,14},{14,13},{17,18},{18,... | collective-permute-start | bytes 393224 | tf_op jit(solution)/shard_map/ppermute | solution.py:445
  7.1 10.3 %collective-permute-start = (f32[16,1024]{1,0:T(8,128)S(1)}, f32[16,1024]{1,0:T(8,128)S(1)}, u32[]{:S(2)}, u32[]{:S(2)}) collective-permute-start(f32[16,1024]{1,0:T(8,128)S(1)} %get-tuple-element.36), channel_id=1, source_target_pairs={{0,4},{4,0},{1,5},{5,1},{2,6},{6,2},{3,7},{7,3},{8,12},{12,8},{9,1... | collective-permute-start | bytes 196616 | tf_op jit(solution)/shard_map/ppermute | solution.py:442
  7.2 10.2 %collective-permute-start.1 = (f32[16,1024]{1,0:T(8,128)S(1)}, f32[16,1024]{1,0:T(8,128)S(1)}, u32[]{:S(2)}, u32[]{:S(2)}) collective-permute-start(f32[16,1024]{1,0:T(8,128)S(1)} %get-tuple-element.37), channel_id=1, source_target_pairs={{4,8},{8,4},{12,16},{16,12},{20,24},{24,20},{28,32},{32,28},{36,40... | collective-permute-start | bytes 196616 | tf_op jit(solution)/shard_map/ppermute | solution.py:443
  20.1 18.3 %all-to-all-start = ((f32[64,1,640]{2,1,0:T(1,128)}), f32[64,1,640]{2,1,0:T(1,128)S(1)}, u32[]{:S(2)}, u32[]{:S(2)}) async-start(f32[64,1,640]{2,1,0:T(1,128)} %get-tuple-element.40), calls=%async_computation | async-start | bytes 327680 | tf_op jit(solution)/shard_map/all_to_all | solution.py:489
  39.1 18.4 %all-to-all-start.1 = ((f32[64,1,640]{2,1,0:T(1,128)}), f32[64,1,640]{2,1,0:T(1,128)S(1)}, u32[]{:S(2)}, u32[]{:S(2)}) async-start(f32[64,1,640]{2,1,0:T(1,128)} %scan.1), calls=%async_computation.1 | async-start | bytes 327680 | tf_op jit(solution)/shard_map/all_to_all | solution.py:522
  47.5 10.0 %collective-permute-start.6 = (f32[32,1,1024]{2,1,0:T(1,128)S(1)}, f32[32,1,1024]{2,1,0:T(1,128)S(1)}, u32[]{:S(2)}, u32[]{:S(2)}) collective-permute-start(f32[32,1,1024]{2,1,0:T(1,128)S(1)} %get-tuple-element.50), channel_id=1, source_target_pairs={{0,1},{1,0},{2,3},{3,2},{4,5},{5,4},{6,7},{7,6},{8,9},{9,8},{10,11... | collective-permute-start | bytes 393224 | tf_op jit(solution)/shard_map/ppermute | solution.py:444
  47.6 9.9 %collective-permute-start.7 = (f32[32,1,1024]{2,1,0:T(1,128)S(1)}, f32[32,1,1024]{2,1,0:T(1,128)S(1)}, u32[]{:S(2)}, u32[]{:S(2)}) collective-permute-start(f32[32,1,1024]{2,1,0:T(1,128)S(1)} %get-tuple-element.51), channel_id=1, source_target_pairs={{1,2},{2,1},{5,6},{6,5},{9,10},{10,9},{13,14},{14,13},{17,18},{18,... | collective-permute-start | bytes 393224 | tf_op jit(solution)/shard_map/ppermute | solution.py:445
  49.6 5.1 %collective-permute-start.4 = (f32[16,1024]{1,0:T(8,128)S(1)}, f32[16,1024]{1,0:T(8,128)S(1)}, u32[]{:S(2)}, u32[]{:S(2)}) collective-permute-start(f32[16,1024]{1,0:T(8,128)S(1)} %get-tuple-element.48), channel_id=1, source_target_pairs={{0,4},{4,0},{1,5},{5,1},{2,6},{6,2},{3,7},{7,3},{8,12},{12,8},{9,1... | collective-permute-start | bytes 196616 | tf_op jit(solution)/shard_map/ppermute | solution.py:442
  49.8 7.7 %collective-permute-start.5 = (f32[16,1024]{1,0:T(8,128)S(1)}, f32[16,1024]{1,0:T(8,128)S(1)}, u32[]{:S(2)}, u32[]{:S(2)}) collective-permute-start(f32[16,1024]{1,0:T(8,128)S(1)} %get-tuple-element.49), channel_id=1, source_target_pairs={{4,8},{8,4},{12,16},{16,12},{20,24},{24,20},{28,32},{32,28},{36,40... | collective-permute-start | bytes 196616 | tf_op jit(solution)/shard_map/ppermute | solution.py:443

commit v4 on v3

--- a/solution.py
+++ b/solution.py
@@ -76,12 +76,16 @@
         copies.append(pltpu.make_async_copy(dens.at[part], held.at[part], sems.at[b]))
         copies[-1].start()
     colours.start()
+    sums = [jnp.zeros((1, dens.shape[2]), jnp.float32)] * 2
     for b, copy in enumerate(copies):
         copy.wait()
         for k in range(b * PIECE, (b + 1) * PIECE):
             top, bottom = held[k, 0:1, :], held[k, nrow - 1 : nrow, :]
             row_one[k] = jnp.where(row_first, bottom, top)
             row_two[k] = jnp.where(row_first, top, bottom)
+            sums = [sums[0] + top, sums[1] + bottom]
+    row_one[ndep] = jnp.where(row_first, sums[1], sums[0])
+    row_two[ndep] = jnp.where(row_first, sums[0], sums[1])
     first_layer, last_layer = held[0], held[ndep - 1]
     to_near[...] = jnp.where(core_first, last_layer, first_layer)
     to_cross[...] = jnp.where(core_first, first_layer, last_layer)
@@ -157,21 +161,17 @@
 
 def forward_kernel(
     step, place, light, tint, dens, cot, weight, square, lean, totals, near, cross, one, two,
-    packed, ends, rho, colour, rims,
+    packed, ends, rho, colour,
 ):
     ndep, _, ncol = dens.shape
     nc = ncol // LANES
     lights = light[0], light[1], light[2]
     masks = ids()
     outer, beyond = facing(place, near, cross, one, two)
-    rims[...] = jnp.zeros_like(rims)
     colour[...] = totals[1]
 
     def edges(k):
         lows, highs = [beyond(k, c, True) for c in range(nc)], [beyond(k, c, False) for c in range(nc)]
-        for c in range(nc):
-            rims[0, :, col(c)] += lows[c]
-            rims[1, :, col(c)] += highs[c]
         return lows, highs
 
     def outermost(k, before, after):
@@ -207,7 +207,9 @@
     )
     pl.loop(1, ndep - 1, unroll=10)(layer)
 
-    passed = [1.0 - absorbed(rims[n] * step, 7) for n in range(2)]
+    row_first = place[1] == 0
+    sums = jnp.where(row_first, two[ndep], one[ndep]), jnp.where(row_first, one[ndep], two[ndep])
+    passed = [1.0 - absorbed(total * step, 7) for total in sums]
     for c in range(nc):
         cs = slice(c * LANES, (c + 1) * LANES)
         for h in range(2):
@@ -452,13 +454,13 @@
         return pltpu.HBM(shape, jnp.float32)
 
     cube, layer, rim = (ndep, nrow, ncol), (nrow, ncol), (ndep, 1, ncol)
-    share = (slabs, 1, 5 * LANES)
+    share, summed = (slabs, 1, 5 * LANES), (ndep + 1, 1, ncol)
     blocks = ndep // BLOCK
     cells = ndep * nrow * ncol
     sem = pltpu.SemaphoreType.DMA
     held, held_cot, *pieces = pl.pallas_call(
         gather_kernel,
-        out_shape=(vmem(*cube), vmem(*cotangent.shape), vmem(*rim), vmem(*rim), vmem(*layer), vmem(*layer)),
+        out_shape=(vmem(*cube), vmem(*cotangent.shape), vmem(*summed), vmem(*summed), vmem(*layer), vmem(*layer)),
         in_specs=[SM, HBM, HBM],
         out_specs=[VM] * 6,
         scratch_shapes=[sem((ndep // PIECE,)), sem],
@@ -480,7 +482,7 @@
         out_shape=(vmem(*share), vmem(2, *layer), vmem(*layer)),
         in_specs=[SM, SM, SM] + [VM] * 10,
         out_specs=[VM] * 3,
-        scratch_shapes=[vmem(*layer), vmem(2, 1, ncol)],
+        scratch_shapes=[vmem(*layer)],
         compiler_params=params(4),
         cost_estimate=cost(30 * cells, 4 * cells),
         name="forward",

time: 62.6 us -> 62.6 us (level)
  no operation moved by 1% of the time
where the time goes in v4:
time: 62.6 us; the launch traced here: 61.7 us
  starting transfers between devices  37.3 us (60%)
  Pallas kernels  19.3 us (31%)
  waiting for transfers between devices  4.79 us (8%)
    ppermute x2, starting transfers between devices, exchange(): lax.ppermute(to_cross, RAY, pairs(1, slabs))  12.9 us
    all_to_all x1, starting transfers between devices, local(): scanned = lax.all_to_all(packed, RAY, 0, 0)  8.73 us
    all_to_all x1, starting transfers between devices, local(): scanned = lax.all_to_all(scanned, RAY, 0, 0)  8.46 us
    pallas_call x1, Pallas kernels, local(): pl.pallas_call(functools.partial(adjoint_kernel, step, full_depth), out_s...  7.65 us
    ppermute x2, starting transfers between devices, exchange(): lax.ppermute(row_two, 'row', pairs(1, rows))  6.23 us
    pallas_call x1, Pallas kernels, local(): pl.pallas_call(functools.partial(combine_kernel, step, full_depth), out_s...  4.12 us
    ppermute x2, waiting for transfers between devices, exchange(): lax.ppermute(to_cross, RAY, pairs(1, slabs))  2.91 us
    pallas_call x1, Pallas kernels, local(): pl.pallas_call(functools.partial(forward_kernel, step), out_shape=(vmem(*...  2.53 us
  transfers between devices with their start and end apart: 10, of which 2 were waited for; matrix products, arithmetic and copies ran while one was open for 0% of the time, Pallas kernels for 16%

profile of v4, /device:TPU:14, one launch (start us, length us, event | category | flops | bytes accessed | tf_op | source)
XLA Modules:
  0.0 61.7 jit_solution(7981900154105125425)
XLA Ops:
  0.0 0.1 pad_add_fusion.place
  0.1 2.2 %gather.1 = (f32[32,16,1024]{2,1,0:T(8,128)S(1)}, f32[3,16,1024]{2,1,0:T(8,128)S(1)}, f32[33,1,1024]{2,1,0:T(1,128)S(1)}, f32[33,1,1024]{2,1,0:T(1,128)S(1)}, f3...) custom-call(s32[2]{0:T(128)S(1)} %pad_add_fusion.place, f32[32,16,1024]{2,1,0:T(8,128)} %dens.3, f32[3,16,1024]{2,1,0:T(8,128)} %cot.1), custom_call_target="tpu_custom_call" | custom-call | tf_op jit(solution)/shard_map/gather/pallas_call | solution.py:461
  2.3 0.5 collective-permute-start.2
  2.8 4.3 %collective-permute-start.3 = (f32[33,1,1024]{2,1,0:T(1,128)S(1)}, f32[33,1,1024]{2,1,0:T(1,128)S(1)}, u32[]{:S(2)}, u32[]{:S(2)}) collective-permute-start(f32[33,1,1024]{2,1,0:T(1,128)S(1)} %get-tuple-element.39), channel_id=1, source_target_pairs={{1,2},{2,1},{5,6},{6,5},{9,10},{10,9},{13,14},{14,13},{17,18},{18,... | collective-permute-start | bytes 405512 | tf_op jit(solution)/shard_map/ppermute | solution.py:447
  7.1 0.1 collective-permute-start
  7.2 8.1 %collective-permute-start.1 = (f32[16,1024]{1,0:T(8,128)S(1)}, f32[16,1024]{1,0:T(8,128)S(1)}, u32[]{:S(2)}, u32[]{:S(2)}) collective-permute-start(f32[16,1024]{1,0:T(8,128)S(1)} %get-tuple-element.37), channel_id=1, source_target_pairs={{4,8},{8,4},{12,16},{16,12},{20,24},{24,20},{28,32},{32,28},{36,40... | collective-permute-start | bytes 196616 | tf_op jit(solution)/shard_map/ppermute | solution.py:445
  15.4 2.0 %inner.1 = (f32[32,16,1024]{2,1,0:T(8,128)S(1)}, f32[32,16,1024]{2,1,0:T(8,128)S(1)}, f32[32,16,1024]{2,1,0:T(8,128)S(1)}, f32[2,16,1024]{2,1,0:T(8,128)S(1)}) custom-call(f32[3]{0:T(128)S(1)} %copy-done, f32[32,16,1024]{2,1,0:T(8,128)S(1)} %get-tuple-element.30.dens), custom_call_target="tpu_custom_call" | custom-call | flops 26214400 | bytes 8388608 | tf_op jit(solution)/shard_map/inner/pallas_call | solution.py:471
  17.4 0.0 collective-permute-done.near
  17.4 0.0 collective-permute-done.1.cross
  17.4 0.0 collective-permute-done.2.one
  17.4 0.0 collective-permute-done.3.two
  17.5 2.5 %forward.1 = (f32[64,1,640]{2,1,0:T(1,128)}, f32[2,16,1024]{2,1,0:T(8,128)S(1)}, f32[16,1024]{1,0:T(8,128)S(1)}) custom-call(s32[2]{0:T(128)S(1)} %pad_add_fusion.place, f32[3]{0:T(128)S(1)} %copy-done, f32[3]{0:T(128)S(1)} %copy-done.1, f32[32,16,1024]{2,1,0:T(8,128)S(1)} %get-tuple-element.30.dens, f32[3,16,1024]{2,1,0:T(8,128)S(1)} %get-tuple-element.31.cot, ...), custom_call_target="tpu_custom_call" | custom-call | flops 15728640 | bytes 2097152 | tf_op jit(solution)/shard_map/forward/pallas_call | solution.py:480
  20.0 8.7 %all-to-all-start = ((f32[64,1,640]{2,1,0:T(1,128)}), f32[64,1,640]{2,1,0:T(1,128)S(1)}, u32[]{:S(2)}, u32[]{:S(2)}) async-start(f32[64,1,640]{2,1,0:T(1,128)} %get-tuple-element.40), calls=%async_computation | async-start | bytes 327680 | tf_op jit(solution)/shard_map/all_to_all | solution.py:491
  28.7 7.7 %adjoint.1 = (f32[33,16,1024]{2,1,0:T(8,128)S(1)}, f32[32,16,1024]{2,1,0:T(8,128)}, f32[32,16,1024]{2,1,0:T(8,128)}, f32[16,1024]{1,0:T(8,128)S(1)}, f32[16,1024...) custom-call(s32[2]{0:T(128)S(1)} %pad_add_fusion.place, f32[3]{0:T(128)S(1)} %copy-done, ...), custom_call_target="tpu_custom_call" | custom-call | flops 36700160 | bytes 8388608 | tf_op jit(solution)/shard_map/adjoint/pallas_call | solution.py:492
  36.4 1.9 %all-to-all-done.packed = f32[64,1,640]{2,1,0:T(1,128)S(1)} async-done(((f32[64,1,640]{2,1,0:T(1,128)}), f32[64,1,640]{2,1,0:T(1,128)S(1)}, u32[]{:S(2)}, u32[]{:S(2)}) %all-to-all-start) | async-done | bytes 163872 | tf_op jit(solution)/shard_map/all_to_all | solution.py:491
  38.3 0.8 %scan.1 = f32[64,1,640]{2,1,0:T(1,128)} custom-call(f32[64,1,640]{2,1,0:T(1,128)S(1)} %all-to-all-done.packed), custom_call_target="tpu_custom_call" | custom-call | tf_op jit(solution)/shard_map/scan/pallas_call | solution.py:516
  39.1 8.5 %all-to-all-start.1 = ((f32[64,1,640]{2,1,0:T(1,128)}), f32[64,1,640]{2,1,0:T(1,128)S(1)}, u32[]{:S(2)}, u32[]{:S(2)}) async-start(f32[64,1,640]{2,1,0:T(1,128)} %scan.1), calls=%async_computation.1 | async-start | bytes 327680 | tf_op jit(solution)/shard_map/all_to_all | solution.py:524
  47.5 0.1 collective-permute-start.6
  47.6 1.9 %collective-permute-start.7 = (f32[32,1,1024]{2,1,0:T(1,128)S(1)}, f32[32,1,1024]{2,1,0:T(1,128)S(1)}, u32[]{:S(2)}, u32[]{:S(2)}) collective-permute-start(f32[32,1,1024]{2,1,0:T(1,128)S(1)} %get-tuple-element.51), channel_id=1, source_target_pairs={{1,2},{2,1},{5,6},{6,5},{9,10},{10,9},{13,14},{14,13},{17,18},{18,... | collective-permute-start | bytes 393224 | tf_op jit(solution)/shard_map/ppermute | solution.py:447
  49.6 0.2 collective-permute-start.4
  49.8 4.8 %collective-permute-start.5 = (f32[16,1024]{1,0:T(8,128)S(1)}, f32[16,1024]{1,0:T(8,128)S(1)}, u32[]{:S(2)}, u32[]{:S(2)}) collective-permute-start(f32[16,1024]{1,0:T(8,128)S(1)} %get-tuple-element.49), channel_id=1, source_target_pairs={{4,8},{8,4},{12,16},{16,12},{20,24},{24,20},{28,32},{32,28},{36,40... | collective-permute-start | bytes 196616 | tf_op jit(solution)/shard_map/ppermute | solution.py:445
  54.6 2.9 %collective-permute-done.5.x_cross = f32[16,1024]{1,0:T(8,128)S(1)} collective-permute-done((f32[16,1024]{1,0:T(8,128)S(1)}, f32[16,1024]{1,0:T(8,128)S(1)}, u32[]{:S(2)}, u32[]{:S(2)}) %collective-permute-start.5) | collective-permute-done | bytes 65568 | tf_op jit(solution)/shard_map/ppermute | solution.py:445
  57.5 0.0 collective-permute-done.6.y_one
  57.5 4.1 %combine.1 = f32[32,16,1024]{2,1,0:T(8,128)} custom-call(s32[2]{0:T(128)S(1)} %pad_add_fusion.place, f32[64,1,640]{2,1,0:T(1,128)S(1)} %all-to-all-done.1.scanned, f32[16,1024]{1,0:T(8,128)S(1)} %collective-permute-done.4.x_near, f32[16,1024]{1,0:T(8,128)S(1)} %collective-permute-done.5.x_cross, f32[32,1,1024]{2,1,0:T(1,128)S(1)} %collective-permute-done.6.y_one, ...), custom_call_target="tpu_custom_call" | custom-call | flops 6291456 | bytes 8388608 | tf_op jit(solution)/shard_map/combine/pallas_call | solution.py:526
  (7 shorter events, 0.0 us)
Async XLA Ops:
  0.0 15.3 %copy-start = (f32[3]{0:T(128)S(1)}, f32[3]{0:T(128)}, u32[]{:S(2)}) copy-start(f32[3]{0:T(128)} %light.5) | copy-start | bytes 40
  0.1 17.4 %copy-start.1 = (f32[3]{0:T(128)S(1)}, f32[3]{0:T(128)}, u32[]{:S(2)}) copy-start(f32[3]{0:T(128)} %tint.1) | copy-start | bytes 40
  2.3 15.2 %collective-permute-start.2 = (f32[33,1,1024]{2,1,0:T(1,128)S(1)}, f32[33,1,1024]{2,1,0:T(1,128)S(1)}, u32[]{:S(2)}, u32[]{:S(2)}) collective-permute-start(f32[33,1,1024]{2,1,0:T(1,128)S(1)} %get-tuple-element.38), channel_id=1, source_target_pairs={{0,1},{1,0},{2,3},{3,2},{4,5},{5,4},{6,7},{7,6},{8,9},{9,8},{10,11... | collective-permute-start | bytes 405512 | tf_op jit(solution)/shard_map/ppermute | solution.py:446
  2.8 14.6 %collective-permute-start.3 = (f32[33,1,1024]{2,1,0:T(1,128)S(1)}, f32[33,1,1024]{2,1,0:T(1,128)S(1)}, u32[]{:S(2)}, u32[]{:S(2)}) collective-permute-start(f32[33,1,1024]{2,1,0:T(1,128)S(1)} %get-tuple-element.39), channel_id=1, source_target_pairs={{1,2},{2,1},{5,6},{6,5},{9,10},{10,9},{13,14},{14,13},{17,18},{18,... | collective-permute-start | bytes 405512 | tf_op jit(solution)/shard_map/ppermute | solution.py:447
  7.1 10.3 %collective-permute-start = (f32[16,1024]{1,0:T(8,128)S(1)}, f32[16,1024]{1,0:T(8,128)S(1)}, u32[]{:S(2)}, u32[]{:S(2)}) collective-permute-start(f32[16,1024]{1,0:T(8,128)S(1)} %get-tuple-element.36), channel_id=1, source_target_pairs={{0,4},{4,0},{1,5},{5,1},{2,6},{6,2},{3,7},{7,3},{8,12},{12,8},{9,1... | collective-permute-start | bytes 196616 | tf_op jit(solution)/shard_map/ppermute | solution.py:444
  7.2 10.2 %collective-permute-start.1 = (f32[16,1024]{1,0:T(8,128)S(1)}, f32[16,1024]{1,0:T(8,128)S(1)}, u32[]{:S(2)}, u32[]{:S(2)}) collective-permute-start(f32[16,1024]{1,0:T(8,128)S(1)} %get-tuple-element.37), channel_id=1, source_target_pairs={{4,8},{8,4},{12,16},{16,12},{20,24},{24,20},{28,32},{32,28},{36,40... | collective-permute-start | bytes 196616 | tf_op jit(solution)/shard_map/ppermute | solution.py:445
  20.0 18.3 %all-to-all-start = ((f32[64,1,640]{2,1,0:T(1,128)}), f32[64,1,640]{2,1,0:T(1,128)S(1)}, u32[]{:S(2)}, u32[]{:S(2)}) async-start(f32[64,1,640]{2,1,0:T(1,128)} %get-tuple-element.40), calls=%async_computation | async-start | bytes 327680 | tf_op jit(solution)/shard_map/all_to_all | solution.py:491
  39.1 18.5 %all-to-all-start.1 = ((f32[64,1,640]{2,1,0:T(1,128)}), f32[64,1,640]{2,1,0:T(1,128)S(1)}, u32[]{:S(2)}, u32[]{:S(2)}) async-start(f32[64,1,640]{2,1,0:T(1,128)} %scan.1), calls=%async_computation.1 | async-start | bytes 327680 | tf_op jit(solution)/shard_map/all_to_all | solution.py:524
  47.5 10.0 %collective-permute-start.6 = (f32[32,1,1024]{2,1,0:T(1,128)S(1)}, f32[32,1,1024]{2,1,0:T(1,128)S(1)}, u32[]{:S(2)}, u32[]{:S(2)}) collective-permute-start(f32[32,1,1024]{2,1,0:T(1,128)S(1)} %get-tuple-element.50), channel_id=1, source_target_pairs={{0,1},{1,0},{2,3},{3,2},{4,5},{5,4},{6,7},{7,6},{8,9},{9,8},{10,11... | collective-permute-start | bytes 393224 | tf_op jit(solution)/shard_map/ppermute | solution.py:446
  47.6 9.9 %collective-permute-start.7 = (f32[32,1,1024]{2,1,0:T(1,128)S(1)}, f32[32,1,1024]{2,1,0:T(1,128)S(1)}, u32[]{:S(2)}, u32[]{:S(2)}) collective-permute-start(f32[32,1,1024]{2,1,0:T(1,128)S(1)} %get-tuple-element.51), channel_id=1, source_target_pairs={{1,2},{2,1},{5,6},{6,5},{9,10},{10,9},{13,14},{14,13},{17,18},{18,... | collective-permute-start | bytes 393224 | tf_op jit(solution)/shard_map/ppermute | solution.py:447
  49.6 5.1 %collective-permute-start.4 = (f32[16,1024]{1,0:T(8,128)S(1)}, f32[16,1024]{1,0:T(8,128)S(1)}, u32[]{:S(2)}, u32[]{:S(2)}) collective-permute-start(f32[16,1024]{1,0:T(8,128)S(1)} %get-tuple-element.48), channel_id=1, source_target_pairs={{0,4},{4,0},{1,5},{5,1},{2,6},{6,2},{3,7},{7,3},{8,12},{12,8},{9,1... | collective-permute-start | bytes 196616 | tf_op jit(solution)/shard_map/ppermute | solution.py:444
  49.8 7.7 %collective-permute-start.5 = (f32[16,1024]{1,0:T(8,128)S(1)}, f32[16,1024]{1,0:T(8,128)S(1)}, u32[]{:S(2)}, u32[]{:S(2)}) collective-permute-start(f32[16,1024]{1,0:T(8,128)S(1)} %get-tuple-element.49), channel_id=1, source_target_pairs={{4,8},{8,4},{12,16},{16,12},{20,24},{24,20},{28,32},{32,28},{36,40... | collective-permute-start | bytes 196616 | tf_op jit(solution)/shard_map/ppermute | solution.py:445
